TPU v7x, 512 devices: a whole 4x4x16 slice. The times are simulated.
512 devices in a mesh: ctx: 128 (over x, z, core), tp: 4 (over y).
Axes of the slice: x: 4, y: 4, z: 16, core: 2. Of those that a mesh axis runs over, the one named last changes fastest.
Arguments:
- query: bfloat16 [16384, 4096], P('ctx', 'tp'), may hold values from -6 to 6
- key_gate: bfloat16 [16384, 4096], P('ctx', 'tp'), may hold values from -6 to 6
- value: bfloat16 [16384, 4096], P('ctx', 'tp'), may hold values from -6 to 6
- cotangent: bfloat16 [16384, 4096], P('ctx', 'tp'), may hold values from -6 to 6
- decay: float32 [4096, 16], P('tp'), as said below
- residue: float32 [4096, 16], P('tp')
Outputs:
- mixed: bfloat16 [16384, 4096], P('ctx', 'tp')
- grad_query: bfloat16 [16384, 4096], P('ctx', 'tp')
- grad_key: bfloat16 [16384, 4096], P('ctx', 'tp')
- grad_value: bfloat16 [16384, 4096], P('ctx', 'tp')
- grad_residue: float32 [4096, 16], P('tp')
Inputs may be any that keep to these rules, and one draw needn't show every extreme that they name: decay lies strictly between 0 and 1.
All inputs are finite; a program needn't handle non-finite values.
Results may differ from a plain program's by a relative error of at most 0.0017.
Values sent between devices are 32-bit elements; how exact they have to be, the bound alone decides.
No kernel may reach another device: no remote copies, remote signals or barrier semaphores. Data moves between devices by JAX's collectives and lax.ppermute only.
A program may use at most 128 MiB of HBM per device.

v0:
```python
import jax
import jax.numpy as jnp
from jax import lax
from jax.sharding import PartitionSpec as P


def from_behind(block, axis, distance):
    devices = range(lax.axis_size(axis))
    route = [(i - distance, i) for i in devices if i - distance in devices]
    return lax.ppermute(block, axis, route)


def shift_down(block_rows, lag):
    if lag == 0:
        return block_rows
    filler = jnp.zeros((block_rows.shape[0], lag, block_rows.shape[2]), jnp.float32)
    return jnp.concatenate([filler, block_rows[:, : block_rows.shape[1] - lag]], axis=1)


def shift_up(block_rows, lag):
    if lag == 0:
        return block_rows
    filler = jnp.zeros((block_rows.shape[0], lag, block_rows.shape[2]), jnp.float32)
    return jnp.concatenate([block_rows[:, lag:], filler], axis=1)


def local(query, key_gate, value, cotangent, decay, residue):
    rows, width = query.shape
    states = decay.shape[1]
    sub = min(16, rows)
    blocks = rows // sub
    dec = decay.T
    logd = jnp.log(dec)
    res = residue.T
    q = query.astype(jnp.float32)
    k = key_gate.astype(jnp.float32)
    v = value.astype(jnp.float32)
    dy = cotangent.astype(jnp.float32)
    gated = (k * v).reshape(blocks, sub, width)
    back = (dy * q).reshape(blocks, sub, width)
    lags = jnp.arange(sub, dtype=jnp.float32)
    powers = jnp.exp(lags[:, None, None] * logd[None])
    kernel = jnp.sum(res[None] * powers, axis=1)
    local_convolution = jnp.zeros((blocks, sub, width), jnp.float32)
    reverse_local = jnp.zeros((blocks, sub, width), jnp.float32)
    lag_sums = []
    for lag in range(sub):
        earlier_rows = shift_down(gated, lag)
        later_rows = shift_up(back, lag)
        local_convolution = local_convolution + kernel[lag][None, None, :] * earlier_rows
        reverse_local = reverse_local + kernel[lag][None, None, :] * later_rows
        lag_sums.append(jnp.sum(back * earlier_rows, axis=(0, 1)))
    lag_indexed = jnp.stack(lag_sums, axis=0)
    end_states = jnp.zeros((blocks, states, width), jnp.float32)
    start_states = jnp.zeros((blocks, states, width), jnp.float32)
    for place in range(sub):
        end_states = end_states + powers[sub - 1 - place][None] * gated[:, place][:, None, :]
        start_states = start_states + powers[place][None] * back[:, place][:, None, :]
    stride = jnp.exp(sub * logd)

    def advance_forward(carry, item):
        return (stride * carry + item, carry)

    zeros = jnp.zeros((states, width), jnp.float32)
    last_fwd, inner_fwd = lax.scan(advance_forward, zeros, end_states)
    last_bwd, inner_bwd = lax.scan(advance_forward, zeros, start_states[::-1])
    inner_bwd = inner_bwd[::-1]
    span = jnp.exp(rows * logd)

    def pass_forward(step, incoming):
        return from_behind(span * incoming + last_fwd, "ctx", 1)

    def pass_backward(step, incoming):
        return from_behind(span * incoming + last_bwd, "ctx", -1)

    prior_value = lax.fori_loop(0, lax.axis_size("ctx") - 1, pass_forward, zeros)
    after = lax.fori_loop(0, lax.axis_size("ctx") - 1, pass_backward, zeros)
    order = jnp.arange(blocks, dtype=jnp.float32)
    total_fwd = inner_fwd + jnp.exp(order[:, None, None] * sub * logd[None]) * prior_value[None]
    total_bwd = (
        inner_bwd + jnp.exp((blocks - 1 - order)[:, None, None] * sub * logd[None]) * after[None]
    )
    lead = jnp.exp((lags + 1.0)[:, None, None] * logd[None])
    trail = jnp.exp((sub - lags)[:, None, None] * logd[None])
    conv = local_convolution
    rev = reverse_local
    weighted_back = jnp.zeros((blocks, states, width), jnp.float32)
    for place in range(sub):
        weighted_back = weighted_back + back[:, place][:, None, :] * lead[place][None]
    for mode in range(states):
        lead_mode = res[mode][None, :] * lead[:, mode]
        trail_mode = res[mode][None, :] * trail[:, mode]
        conv = conv + lead_mode[None] * total_fwd[:, mode][:, None, :]
        rev = rev + trail_mode[None] * total_bwd[:, mode][:, None, :]
    conv = conv.reshape(rows, width)
    rev = rev.reshape(rows, width)
    inside = jnp.sum(powers * lag_indexed[:, None, :], axis=0)
    carried = jnp.sum(weighted_back * total_fwd, axis=0)
    grad_residue = lax.psum(inside + carried, "ctx").T
    mixed = (q * conv).astype(jnp.bfloat16)
    grad_query = (dy * conv).astype(jnp.bfloat16)
    grad_key = (rev * v).astype(jnp.bfloat16)
    grad_value = (rev * k).astype(jnp.bfloat16)
    return (mixed, grad_query, grad_key, grad_value, grad_residue)


def solution(mesh):
    in_specs = (
        P("ctx", "tp"),
        P("ctx", "tp"),
        P("ctx", "tp"),
        P("ctx", "tp"),
        P("tp", None),
        P("tp", None),
    )
    out_specs = (P("ctx", "tp"), P("ctx", "tp"), P("ctx", "tp"), P("ctx", "tp"), P("tp", None))
    return jax.shard_map(local, mesh=mesh, in_specs=in_specs, out_specs=out_specs, check_vma=False)
```

profile of v0, /device:TPU:6, one launch (start us, length us, event | category | flops | bytes accessed | tf_op | source)
XLA Modules:
  0.0 2058.5 jit_solution(2534971427344696478)
XLA Ops:
  26.9 12.1 while.48
  45.0 984.7 %while.46 = (s32[]{:T(128)}, f32[16,1024]{1,0:T(8,128)S(1)}, f32[16,1024]{1,0:T(8,128)S(1)}, f32[16,1024]{1,0:T(8,128)S(1)}, s32[]{:T(128)}) while((s32[]{:T(128)}, f32[16,1024]{1,0:T(8,128)S(1)}, f32[16,1024]{1,0:T(8,128)S(1)}, f32[16,1024]{1,0:T(8,128)S(1)}, s32[]{:T(128)}) %tuple.268), condition=%wide.region_4.0_spmd, body=%wide.region_3.0_spmd.sunk | while | flops 32770 | bytes 524389 | solution.py:76
  46.9 11.1 collective-permute-done
  1067.5 976.0 %while.47 = (s32[]{:T(128)}, f32[16,1024]{1,0:T(8,128)S(1)}, f32[16,1024]{1,0:T(8,128)S(1)}, f32[16,1024]{1,0:T(8,128)S(1)}, s32[]{:T(128)}) while((s32[]{:T(128)}, f32[16,1024]{1,0:T(8,128)S(1)}, f32[16,1024]{1,0:T(8,128)S(1)}, f32[16,1024]{1,0:T(8,128)S(1)}, s32[]{:T(128)}) %tuple.280), condition=%wide.region_8.0_spmd, body=%wide.region_7.0_spmd.sunk | while | flops 32770 | bytes 524389 | solution.py:77
  1071.5 5.8 collective-permute-start.1
  1079.2 5.8 collective-permute-start.1
  1086.9 5.8 collective-permute-start.1
  1094.6 5.8 collective-permute-start.1
  1102.3 5.8 collective-permute-start.1
  1110.1 5.8 collective-permute-start.1
  1117.8 5.8 collective-permute-start.1
  1125.5 5.8 collective-permute-start.1
  1133.2 5.8 collective-permute-start.1
  1140.9 5.8 collective-permute-start.1
  1148.7 5.9 collective-permute-start.1
  1156.4 5.8 collective-permute-start.1
  1164.2 5.8 collective-permute-start.1
  1171.9 5.8 collective-permute-start.1
  1179.7 5.8 collective-permute-start.1
  1187.4 5.8 collective-permute-start.1
  1195.1 5.8 collective-permute-start.1
  1202.8 5.8 collective-permute-start.1
  1210.5 5.8 collective-permute-start.1
  1218.3 5.8 collective-permute-start.1
  1226.0 5.8 collective-permute-start.1
  1233.7 5.8 collective-permute-start.1
  1241.5 5.8 collective-permute-start.1
  1249.2 5.8 collective-permute-start.1
  1264.6 5.8 collective-permute-start.1
  1272.3 5.8 collective-permute-start.1
  1280.0 5.8 collective-permute-start.1
  1287.8 5.8 collective-permute-start.1
  1295.5 5.8 collective-permute-start.1
  1303.2 5.8 collective-permute-start.1
  1310.9 5.8 collective-permute-start.1
  1318.7 5.8 collective-permute-start.1
  1326.4 5.8 collective-permute-start.1
  1341.8 5.8 collective-permute-start.1
  1349.5 5.8 collective-permute-start.1
  1357.2 5.8 collective-permute-start.1
  1364.9 5.8 collective-permute-start.1
  1372.6 5.8 collective-permute-start.1
  1380.4 5.8 collective-permute-start.1
  1388.1 5.8 collective-permute-start.1
  1403.5 5.8 collective-permute-start.1
  1411.2 5.8 collective-permute-start.1
  1418.9 5.8 collective-permute-start.1
  1426.6 5.8 collective-permute-start.1
  1434.3 5.8 collective-permute-start.1
  1442.0 5.8 collective-permute-start.1
  1449.8 5.8 collective-permute-start.1
  1457.5 5.8 collective-permute-start.1
  1465.2 5.8 collective-permute-start.1
  1472.9 5.8 collective-permute-start.1
  1488.3 5.8 collective-permute-start.1
  1496.0 5.8 collective-permute-start.1
  1503.7 5.8 collective-permute-start.1
  1511.4 5.8 collective-permute-start.1
  1519.2 5.8 collective-permute-start.1
  1526.9 5.8 collective-permute-start.1
  1534.6 5.8 collective-permute-start.1
  1550.0 5.8 collective-permute-start.1
  1557.7 5.8 collective-permute-start.1
  1565.4 5.8 collective-permute-start.1
  (1160 shorter events, 1679.1 us)
Async XLA Ops:
  7.2 2043.0 %all-reduce.32.cloned.1.call-start = ((), (), s32[]{:S(2)}) async-start(), calls=%async_computation | async-start | bytes 131072 | tf_op jit(solution)/shard_map/psum | solution.py:99
  45.0 13.1 collective-permute-start
  1071.5 7.7 collective-permute-start.1
  1079.2 7.7 collective-permute-start.1
  1086.9 7.7 collective-permute-start.1
  1094.6 7.7 collective-permute-start.1
  1102.3 7.7 collective-permute-start.1
  1110.1 7.7 collective-permute-start.1
  1117.8 7.7 collective-permute-start.1
  1125.5 7.7 collective-permute-start.1
  1133.2 7.7 collective-permute-start.1
  1140.9 7.7 collective-permute-start.1
  1148.7 7.8 collective-permute-start.1
  1156.4 7.7 collective-permute-start.1
  1164.2 7.7 collective-permute-start.1
  1171.9 7.7 collective-permute-start.1
  1179.7 7.7 collective-permute-start.1
  1187.4 7.7 collective-permute-start.1
  1195.1 7.7 collective-permute-start.1
  1202.8 7.7 collective-permute-start.1
  1210.5 7.7 collective-permute-start.1
  1218.3 7.7 collective-permute-start.1
  1226.0 7.7 collective-permute-start.1
  1233.7 7.7 collective-permute-start.1
  1241.5 7.7 collective-permute-start.1
  1249.2 7.7 collective-permute-start.1
  1264.6 7.7 collective-permute-start.1
  1272.3 7.7 collective-permute-start.1
  1280.0 7.7 collective-permute-start.1
  1287.8 7.7 collective-permute-start.1
  1295.5 7.7 collective-permute-start.1
  1303.2 7.7 collective-permute-start.1
  1310.9 7.7 collective-permute-start.1
  1318.7 7.7 collective-permute-start.1
  1326.4 7.7 collective-permute-start.1
  1341.8 7.7 collective-permute-start.1
  1349.5 7.7 collective-permute-start.1
  1357.2 7.7 collective-permute-start.1
  1364.9 7.7 collective-permute-start.1
  1372.6 7.7 collective-permute-start.1
  1380.4 7.7 collective-permute-start.1
  1388.1 7.7 collective-permute-start.1
  1403.5 7.7 collective-permute-start.1
  1411.2 7.7 collective-permute-start.1
  1418.9 7.7 collective-permute-start.1
  1426.6 7.7 collective-permute-start.1
  1434.3 7.7 collective-permute-start.1
  1442.0 7.7 collective-permute-start.1
  1449.8 7.7 collective-permute-start.1
  1465.2 7.7 collective-permute-start.1
  1472.9 7.7 collective-permute-start.1
  1488.3 7.7 collective-permute-start.1
  1496.0 7.7 collective-permute-start.1
  1503.7 7.7 collective-permute-start.1
  1511.4 7.7 collective-permute-start.1
  1519.2 7.7 collective-permute-start.1
  1526.9 7.7 collective-permute-start.1
  1534.6 7.7 collective-permute-start.1
  1550.0 7.7 collective-permute-start.1
  1557.7 7.7 collective-permute-start.1
  1565.4 7.7 collective-permute-start.1
  1573.1 7.7 collective-permute-start.1
  1580.8 7.7 collective-permute-start.1
  1588.6 7.7 collective-permute-start.1
  (336 other events, 2852.2 us)
Sparse Core Ops, SparseCore 0:
  1034.4 300.9 all-reduce.31
where the time goes:
time: 2080 us; the launch traced here: 2060 us
  starting transfers between devices  978 us (47%)
  waiting for transfers between devices  976 us (47%)
  local copies, waits for them, and re-layouts  47.9 us (2%)
  other arithmetic  36.8 us (2%)
    ppermute x254, starting transfers between devices, from_behind(): return lax.ppermute(block, axis, route)  978 us
    ppermute x254, waiting for transfers between devices, from_behind(): return lax.ppermute(block, axis, route)  976 us
  transfers between devices with their start and end apart: 255, of which 254 were waited for; matrix products, arithmetic and copies ran while one was open for 1% of the time, Pallas kernels for 0%

commit v1 on v0

v1 whole, which is shorter than its diff:
```python
import functools

import jax
import jax.numpy as jnp
from jax import lax
from jax.experimental import pallas as pl
from jax.experimental.pallas import tpu as pltpu
from jax.sharding import PartitionSpec as P

LANES = 128
SUBS = 8
WIDTH = 4
DEPTH = 16


def listing(first, depths):
    chips = [x * DEPTH + z for z in depths for x in range(WIDTH)]
    return [first] + [chip for chip in chips if chip != first]


OUT = listing(2 * DEPTH + 11, sorted(range(DEPTH), key=lambda z: min(z, DEPTH - z)))
BACK = listing(2 * DEPTH + 8, range(DEPTH))


def runs(order, start):
    slots = [order.index(row % WIDTH * DEPTH + row // WIDTH) for row in range(start, start + SUBS)]
    found = []
    for place, slot in enumerate(slots):
        if found and slot == found[-1][1] + found[-1][2]:
            found[-1][2] += 1
        else:
            found.append([place, slot, 1])
    return found
CHUNK = 32


def register(ref, index):
    return ref[pl.ds(pl.multiple_of(index * SUBS, SUBS), SUBS), :]


def spread_modes(source_ref, scratch):
    for mode in range(0, source_ref.shape[0], SUBS):
        for tile in range(SUBS):
            scratch[pl.ds(mode * SUBS + tile, SUBS, stride=SUBS), :] = source_ref[
                pl.ds(mode, SUBS), pl.ds(tile * LANES, LANES)
            ]


def power(base, exponent):
    for _ in range(exponent.bit_length() - 1):
        base = base * base
    return base


def load_copies(sources, buffers, sems):
    rows = sources[0].shape[0]
    copies = []
    for chunk in range(rows // CHUNK):
        place = pl.ds(chunk * CHUNK, CHUNK)
        copies.append(
            [
                pltpu.make_async_copy(source.at[place, :], buffers.at[item, place, :], sems.at[item, chunk])
                for item, source in enumerate(sources)
            ]
        )
    return copies


def end_states(half, u_ref, e_ref, d_ref, out_ref):
    rows = u_ref.shape[0] // SUBS
    part = out_ref.shape[1] // SUBS
    steps = 8
    dec = [register(d_ref, half * part + mode) for mode in range(part)]
    zeros = (jnp.zeros((SUBS, LANES), jnp.float32),) * part

    def body(step, carry):
        fwd, bwd, inside = (list(item) for item in carry)
        for inner in range(steps):
            row = step * steps + inner
            u = register(u_ref, row)
            e = register(e_ref, row)
            late = register(e_ref, rows - 1 - row)
            for mode in range(part):
                fwd[mode] = dec[mode] * fwd[mode] + u
                bwd[mode] = dec[mode] * bwd[mode] + late
                inside[mode] = inside[mode] + e * fwd[mode]
        return tuple(fwd), tuple(bwd), tuple(inside)

    found = lax.fori_loop(0, rows // steps, body, (zeros, zeros, zeros))
    for which, items in enumerate(found):
        for mode in range(part):
            out_ref[which, pl.ds(mode * SUBS, SUBS), :] = items[mode]


def first_kernel(
    core_ref, q_ref, k_ref, v_ref, dy_ref, dec_ref, theirs_ref, u_ref, e_ref, d_ref,
    buffers, sems, modes, modes_sem,
):
    rows = q_ref.shape[0]
    modes_copy = pltpu.make_async_copy(dec_ref, modes, modes_sem)
    copies = load_copies((q_ref, k_ref, v_ref, dy_ref), buffers, sems)
    for group in copies:
        for copy in group:
            copy.start()
    modes_copy.start()
    for chunk, group in enumerate(copies):
        for copy in group:
            copy.wait()
        for row in range(chunk * CHUNK, (chunk + 1) * CHUNK, 16):
            for tile in range(SUBS):
                here = (pl.ds(row, 16), pl.ds(tile * LANES, LANES))
                q, k, v, dy = (buffers[(item,) + here].astype(jnp.float32) for item in range(4))
                for ref, values in ((u_ref, k * v), (e_ref, dy * q)):
                    for half in range(2):
                        start = (row + half * SUBS) * SUBS + tile
                        ref[pl.ds(start, SUBS, stride=SUBS), :] = values[half * SUBS : (half + 1) * SUBS]
    modes_copy.wait()
    spread_modes(modes, d_ref)
    end_states(1 - core_ref[0], u_ref, e_ref, d_ref, theirs_ref)


def second_kernel(core_ref, u_ref, e_ref, d_ref, mine_ref):
    end_states(core_ref[0], u_ref, e_ref, d_ref, mine_ref)


def chip_kernel(rows, core_ref, mine_ref, got_ref, d_ref, give_ref, edge_ref, after_ref):
    part = mine_ref.shape[1] // SUBS
    first = core_ref[0] == 0
    for mode in range(part):
        place = pl.ds(mode * SUBS, SUBS)
        dec = register(d_ref, core_ref[0] * part + mode)
        span = power(dec, rows)
        here = [mine_ref[which, place, :] for which in range(3)]
        there = [got_ref[which, place, :] for which in range(3)]
        early = [jnp.where(first, a, b) for a, b in zip(here, there)]
        late = [jnp.where(first, b, a) for a, b in zip(here, there)]
        joined = (
            span * early[0] + late[0],
            early[1] + span * late[1],
            early[2] + late[2] + dec * (late[1] * early[0]),
        )
        for begin, slot, size in runs(OUT, mode * SUBS):
            for which in range(3):
                lanes = pl.ds(which * LANES, LANES)
                give_ref[pl.ds(slot, size), 0, lanes] = joined[which][begin : begin + size]
        edge_ref[0, place, :] = early[0]
        edge_ref[1, place, :] = late[1]
    after_ref[...] = jnp.zeros_like(after_ref)


def inner_kernel(
    u_ref, e_ref, d_ref, res_ref, after_ref,
    conv_ref, rev_ref, lead_ref, trail_ref, leap_ref, ready_ref, r_ref, spun,
):
    ready_ref[...] = after_ref[...]
    rows = u_ref.shape[0] // SUBS
    states = res_ref.shape[0]
    spread_modes(res_ref, r_ref)
    dec = [register(d_ref, mode) for mode in range(states)]
    res = [register(r_ref, mode) for mode in range(states)]

    def sweep(values_ref, out_ref, steps, first, direction):
        def body(step, carry):
            state = list(carry)
            for inner in range(steps):
                row = first + direction * (step * steps + inner)
                item = register(values_ref, row)
                terms = []
                for mode in range(states):
                    state[mode] = dec[mode] * state[mode] + item
                    terms.append(res[mode] * state[mode])
                while len(terms) > 1:
                    terms = [a + b for a, b in zip(terms[::2], terms[1::2])]
                spun[pl.ds(pl.multiple_of(row * SUBS, SUBS), SUBS), :] = terms[0]
            return tuple(state)

        zeros = (jnp.zeros((SUBS, LANES), jnp.float32),) * states
        lax.fori_loop(0, rows // steps, body, zeros)

        def settle(group, _):
            row = pl.multiple_of(group * SUBS, SUBS)
            for tile in range(SUBS):
                out_ref[pl.ds(row, SUBS), pl.ds(tile * LANES, LANES)] = spun[
                    pl.ds(row * SUBS + tile, SUBS, stride=SUBS), :
                ]
            return 0

        lax.fori_loop(0, rows // SUBS, settle, 0)

    sweep(u_ref, conv_ref, 4, 0, 1)
    sweep(e_ref, rev_ref, 4, rows - 1, -1)
    place = lax.broadcasted_iota(jnp.int32, (SUBS, LANES), 0)

    def weights(mode, _):
        for tile in range(SUBS):
            lanes = pl.ds(tile * LANES, LANES)
            cell = pl.ds(mode * SUBS + tile, 1)
            one = jnp.broadcast_to(d_ref[cell, :], place.shape)
            lead = one * r_ref[cell, :]
            trail = lead
            for bit in range(3):
                lead = jnp.where((place >> bit) & 1 == 1, lead * one, lead)
                trail = jnp.where((place >> bit) & 1 == 0, trail * one, trail)
                one = one * one
            lead_ref[mode, :, lanes] = lead
            trail_ref[mode, :, lanes] = trail
            leap_ref[cell, :] = one[:1]
        return 0

    lax.fori_loop(0, states, weights, 0)


def chain_kernel(rows, core_ref, row_ref, take_ref, d_ref, after_ref, give_ref):
    count = take_ref.shape[0]
    dec = d_ref[pl.ds(core_ref[0] * count + row_ref[0], 1), :]
    span = power(dec, 2 * rows)
    zeros = jnp.zeros_like(dec)
    first, second, third = (pl.ds(which * LANES, LANES) for which in range(3))
    before, after, inside, cross = zeros, zeros, zeros, zeros
    for chip in range(count):
        source, turned = OUT.index(chip), OUT.index(count - 1 - chip)
        give_ref[BACK.index(chip), :, first] = before
        give_ref[BACK.index(count - 1 - chip), :, second] = after
        inside = inside + take_ref[source, :, third]
        cross = cross + take_ref[source, :, second] * before
        before = span * before + take_ref[source, :, first]
        after = span * after + take_ref[turned, :, second]
    total = inside + dec * cross
    for block in range(count):
        give_ref[block, :, third] = total


def split_kernel(rows, core_ref, take_ref, edge_ref, d_ref, keep_ref, pass_ref, sorted_ref):
    part = edge_ref.shape[1] // SUBS
    first = core_ref[0] == 0
    for mode in range(part):
        place = pl.ds(mode * SUBS, SUBS)
        dec = register(d_ref, core_ref[0] * part + mode)
        span = power(dec, rows)
        stretches = runs(BACK, mode * SUBS)
        found = []
        for which in range(3):
            lanes = pl.ds(which * LANES, LANES)
            if len(stretches) == 1:
                found.append(take_ref[pl.ds(stretches[0][1], SUBS), 0, lanes])
                continue
            for begin, slot, size in stretches:
                sorted_ref[which, pl.ds(begin, size), :] = take_ref[pl.ds(slot, size), 0, lanes]
            found.append(sorted_ref[which])
        start, end, total = found
        middle = span * start + edge_ref[0, place, :]
        turn = span * end + edge_ref[1, place, :]
        keep_ref[0, place, :] = jnp.where(first, start, middle)
        pass_ref[0, place, :] = jnp.where(first, middle, start)
        keep_ref[1, place, :] = jnp.where(first, turn, end)
        pass_ref[1, place, :] = jnp.where(first, end, turn)
        keep_ref[2, place, :] = total
        pass_ref[2, place, :] = total


def edge_terms(half, table_ref, leap_ref, states_ref, which, tile, lanes):
    part = states_ref.shape[1] // SUBS
    terms, leaps = [], []
    for mode in range(part):
        state = states_ref[which, pl.ds(mode * SUBS + tile, 1), :]
        terms.append(table_ref[half * part + mode, :, lanes] * state)
        leaps.append(leap_ref[pl.ds((half * part + mode) * SUBS + tile, 1), :])
    return terms, leaps


def total_of(terms):
    while len(terms) > 1:
        terms = [a + b for a, b in zip(terms[::2], terms[1::2])]
    return terms[0]


def own_kernel(
    core_ref, q_ref, k_ref, v_ref, dy_ref, conv_ref, rev_ref, lead_ref, trail_ref, leap_ref, keep_ref,
    conv_out, rev_out, inputs_out, sems,
):
    copies = load_copies((q_ref, k_ref, v_ref, dy_ref), inputs_out, sems)
    for group in copies:
        for copy in group:
            copy.start()
    groups = conv_ref.shape[0] // SUBS

    def body(tile, _):
        lanes = pl.ds(pl.multiple_of(tile * LANES, LANES), LANES)
        for which, table, source, out in ((0, lead_ref, conv_ref, conv_out), (1, trail_ref, rev_ref, rev_out)):
            terms, leaps = edge_terms(core_ref[0], table, leap_ref, keep_ref, which, tile, lanes)
            for step in range(groups):
                group = step if which == 0 else groups - 1 - step
                here = (pl.ds(group * SUBS, SUBS), lanes)
                out[here] = source[here] + total_of(terms)
                if step < groups - 1:
                    terms = [a * b for a, b in zip(terms, leaps)]
        return 0

    lax.fori_loop(0, SUBS, body, 0)
    for group in copies:
        for copy in group:
            copy.wait()


def mix_kernel(
    core_ref, inputs_ref, conv_ref, rev_ref, lead_ref, trail_ref, leap_ref, keep_ref, got_ref,
    mixed_ref, gq_ref, gk_ref, gv_ref, gr_ref,
    results, out_sems,
):
    rows = conv_ref.shape[0]
    pairs = rows // (2 * SUBS)
    part = keep_ref.shape[1] // SUBS
    other = 1 - core_ref[0]
    ways = (
        (0, lead_ref, conv_ref, (0, 3), (0, 1)),
        (1, trail_ref, rev_ref, (2, 1), (2, 3)),
    )
    outs = (mixed_ref, gq_ref, gk_ref, gv_ref)

    def leaving(item, tile):
        lanes = pl.ds(pl.multiple_of(tile * LANES, LANES), LANES)
        return pltpu.make_async_copy(
            results.at[item, :, lanes], outs[item].at[:, lanes], out_sems.at[item, tile]
        )

    def body(tile, _):
        lanes = pl.ds(pl.multiple_of(tile * LANES, LANES), LANES)
        for which, table, source, factors, targets in ways:
            terms, leaps = edge_terms(other, table, leap_ref, got_ref, which, tile, lanes)
            for step in range(pairs):
                pair = step if which == 0 else pairs - 1 - step
                halves = []
                for order in range(2):
                    half = order if which == 0 else 1 - order
                    here = (pl.ds((2 * pair + half) * SUBS, SUBS), lanes)
                    halves.append(source[here] + total_of(terms))
                    if step < pairs - 1 or order == 0:
                        terms = [a * b for a, b in zip(terms, leaps)]
                values = jnp.concatenate(halves if which == 0 else halves[::-1], axis=0)
                spot = (pl.ds(pair * 2 * SUBS, 2 * SUBS), lanes)
                for factor, target in zip(factors, targets):
                    product = inputs_ref[(factor,) + spot].astype(jnp.float32) * values
                    results[(target,) + spot] = product.astype(jnp.bfloat16)
            for target in targets:
                leaving(target, tile).start()
        return 0

    lax.fori_loop(0, SUBS, body, 0)
    for ref, half in ((keep_ref, core_ref[0]), (got_ref, other)):
        for tile in range(SUBS):
            place = (pl.ds(pl.multiple_of(half * part, SUBS), part), pl.ds(tile * LANES, LANES))
            gr_ref[place] = ref.at[2][pl.ds(tile, part, stride=SUBS), :]
    for tile in range(SUBS):
        for item in range(len(outs)):
            leaving(item, tile).wait()


def local(query, key_gate, value, cotangent, decay, residue):
    rows, width = query.shape
    states = decay.shape[1]
    count = lax.axis_size("ctx")
    chips = count // 2
    cells = states * width // LANES
    dec = decay.T
    res = residue.T

    def members(order):
        return [[2 * chip + core for chip in order] for core in range(2)]

    swap = [(device, device ^ 1) for device in range(count)]
    params = pltpu.CompilerParams(vmem_limit_bytes=24 * 1024 * 1024)

    def array(*shape):
        return jax.ShapeDtypeStruct(shape, jnp.float32)

    wide = array(rows * SUBS, LANES)
    plain = array(rows, width)
    spread = array(cells, LANES)
    table = array(states, SUBS, width)
    halved = array(3, cells // 2, LANES)
    packed = array(chips, 1, 3 * LANES)
    block = jax.ShapeDtypeStruct((rows, width), jnp.bfloat16)
    four = jax.ShapeDtypeStruct((4, rows, width), jnp.bfloat16)
    scalar = pl.BlockSpec(memory_space=pltpu.SMEM)
    vector = pl.BlockSpec(memory_space=pltpu.VMEM)
    remote = pl.BlockSpec(memory_space=pltpu.HBM)

    def run(kernel, name, specs, operands, out_shape, out_specs=None, scratch=(), work=2):
        return pl.pallas_call(
            kernel,
            out_shape=out_shape,
            in_specs=specs,
            out_specs=jax.tree.map(lambda _: vector, out_shape) if out_specs is None else out_specs,
            scratch_shapes=list(scratch),
            compiler_params=params,
            cost_estimate=pl.CostEstimate(
                flops=work * states * rows * width, bytes_accessed=4 * rows * width, transcendentals=0
            ),
            name=name,
        )(*operands)

    index = lax.axis_index("ctx").astype(jnp.int32).reshape(1)
    core = index & 1
    chip = index >> 1
    row = (chip & (DEPTH - 1)) * WIDTH + chip // DEPTH
    inputs = [
        pltpu.with_memory_space_constraint(item, pltpu.HBM)
        for item in (query, key_gate, value, cotangent, dec)
    ]
    loads = pltpu.SemaphoreType.DMA((4, rows // CHUNK))
    theirs, u, e, modes = run(
        first_kernel, "first",
        [scalar] + [remote] * 5, (core, *inputs),
        (halved, wide, wide, spread),
        scratch=(
            pltpu.VMEM(four.shape, four.dtype), loads,
            pltpu.VMEM((states, width), jnp.float32), pltpu.SemaphoreType.DMA,
        ),
        work=6,
    )
    got = lax.ppermute(theirs, "ctx", swap)
    mine = run(second_kernel, "second", [scalar] + [vector] * 3, (core, u, e, modes), halved, work=3)
    send, edge, after = run(
        functools.partial(chip_kernel, rows), "chip",
        [scalar] + [vector] * 3, (core, mine, got, modes),
        (packed, array(2, cells // 2, LANES), array(SUBS, LANES)),
    )
    here = lax.all_to_all(send, "ctx", 0, 0, axis_index_groups=members(OUT), tiled=True)
    conv, rev, lead, trail, leap, ready = run(
        inner_kernel, "inner",
        [vector] * 5, (u, e, modes, res, after),
        (plain, plain, table, table, spread, array(SUBS, LANES)),
        scratch=(pltpu.VMEM(spread.shape, jnp.float32), pltpu.VMEM(wide.shape, jnp.float32)),
        work=8,
    )
    back = run(
        functools.partial(chain_kernel, rows), "chain",
        [scalar] * 2 + [vector] * 3, (core, row, here, modes, ready), packed,
    )
    take = lax.all_to_all(back, "ctx", 0, 0, axis_index_groups=members(BACK), tiled=True)
    keep, away = run(
        functools.partial(split_kernel, rows), "split",
        [scalar] + [vector] * 3, (core, take, edge, modes), (halved, halved),
        scratch=(pltpu.VMEM((3, SUBS, LANES), jnp.float32),),
    )
    arrived = lax.ppermute(away, "ctx", swap)
    conv, rev, held = run(
        own_kernel, "own",
        [scalar] + [remote] * 4 + [vector] * 6,
        (core, *inputs[:4], conv, rev, lead, trail, leap, keep), (plain, plain, four),
        scratch=(loads,),
    )
    mixed, grad_query, grad_key, grad_value, grad_residue = run(
        mix_kernel, "mix",
        [scalar] + [vector] * 8,
        (core, held, conv, rev, lead, trail, leap, keep, arrived),
        (block, block, block, block, array(states, width)),
        out_specs=(remote, remote, remote, remote, vector),
        scratch=(
            pltpu.VMEM((4, rows, width), jnp.bfloat16), pltpu.SemaphoreType.DMA((4, SUBS)),
        ),
    )
    return (mixed, grad_query, grad_key, grad_value, grad_residue.T)


def solution(mesh):
    in_specs = (
        P("ctx", "tp"),
        P("ctx", "tp"),
        P("ctx", "tp"),
        P("ctx", "tp"),
        P("tp", None),
        P("tp", None),
    )
    out_specs = (P("ctx", "tp"), P("ctx", "tp"), P("ctx", "tp"), P("ctx", "tp"), P("tp", None))
    return jax.shard_map(local, mesh=mesh, in_specs=in_specs, out_specs=out_specs, check_vma=False)
```

time: 2080 us -> 62.2 us (0.03)
  the two profiles are of different devices: /device:TPU:6 before, /device:TPU:1 now
where the time goes in v1:
time: 62.2 us; the launch traced here: 61.8 us
  starting transfers between devices  27.2 us (44%)
  blocking collectives  18.5 us (30%)
  Pallas kernels  11.1 us (18%)
  waiting for transfers between devices  4.26 us (7%)
  between operations  0.73 us (1%)
    all_to_all x1, blocking collectives, local(): lax.all_to_all(back, 'ctx', 0, 0, axis_index_groups=members(BACK), tiled=...  18.5 us
    all_to_all x1, starting transfers between devices, local(): lax.all_to_all(send, 'ctx', 0, 0, axis_index_groups=members(OUT), tiled=T...  14 us
    pallas_call x8, Pallas kernels, run(): pl.pallas_call(kernel, out_shape=out_shape, in_specs=specs, out_specs=jax...  11.1 us
    ppermute x1, starting transfers between devices, local(): got = lax.ppermute(theirs, 'ctx', swap)  8.79 us
    ppermute x1, starting transfers between devices, local(): arrived = lax.ppermute(away, 'ctx', swap)  4.39 us
    all_to_all x1, waiting for transfers between devices, local(): lax.all_to_all(send, 'ctx', 0, 0, axis_index_groups=members(OUT), tiled=T...  4.23 us
  transfers between devices with their start and end apart: 3, of which 1 were waited for; matrix products, arithmetic and copies ran while one was open for 0% of the time, Pallas kernels for 9%

profile of v1, /device:TPU:1, one launch (start us, length us, event | category | flops | bytes accessed | tf_op | source)
XLA Modules:
  0.0 61.8 jit_solution(10266914079582145684)
XLA Ops:
  0.6 2.3 %first.1 = (f32[3,64,128]{2,1,0:T(8,128)S(1)}, f32[1024,128]{1,0:T(8,128)S(1)}, f32[1024,128]{1,0:T(8,128)S(1)}, f32[128,128]{1,0:T(8,128)S(1)}) custom-call(s32[1]{0:T(128)} %bitcast.core_ref, bf16[128,1024]{1,0:T(8,128)(2,1)} %q_ref.3, bf16[128,1024]{1,0:T(8,128)(2,1)} %k_ref.3, bf16[128,1024]{1,0:T(8,128)(2,1)} %v_ref.3, bf16[128,1024]{1,0:T(8,128)(2,1)} %dy_ref.3, ...), custom_call_target="tpu_custom_call" | custom-call | flops 12582912 | bytes 524288 | tf_op jit(solution)/shard_map/first/pallas_call | solution.py:389
  3.0 8.8 %collective-permute-start = (f32[3,64,128]{2,1,0:T(8,128)S(1)}, f32[3,64,128]{2,1,0:T(8,128)S(1)}, u32[]{:S(2)}, u32[]{:S(2)}) collective-permute-start(f32[3,64,128]{2,1,0:T(8,128)S(1)} %get-tuple-element.31), channel_id=1, source_target_pairs={{0,4},{4,0},{8,12},{12,8},{16,20},{20,16},{24,28},{28,24},{32,36},... | collective-permute-start | bytes 294920 | tf_op jit(solution)/shard_map/ppermute | solution.py:421
  11.8 0.9 %second.1.mine_ref = f32[3,64,128]{2,1,0:T(8,128)S(1)} custom-call(s32[1]{0:T(128)} %bitcast.core_ref, f32[1024,128]{1,0:T(8,128)S(1)} %get-tuple-element.28.u_ref, f32[1024,128]{1,0:T(8,128)S(1)} %get-tuple-element.29.e_ref, f32[128,128]{1,0:T(8,128)S(1)} %get-tuple-element.30.d_ref), custom_call_target="tpu_custom_call" | custom-call | flops 6291456 | bytes 524288 | tf_op jit(solution)/shard_map/second/pallas_call | solution.py:389
  12.7 0.0 collective-permute-done.got_ref
  12.7 0.7 %chip.1 = (f32[64,1,384]{2,1,0:T(1,128)}, f32[2,64,128]{2,1,0:T(8,128)S(1)}, f32[8,128]{1,0:T(8,128)S(1)}) custom-call(s32[1]{0:T(128)} %bitcast.core_ref, f32[3,64,128]{2,1,0:T(8,128)S(1)} %second.1.mine_ref, f32[3,64,128]{2,1,0:T(8,128)S(1)} %collective-permute-done.got_ref, f32[128,128]{1,0:T(8,128)S(1)} %get-tuple-element.30.d_ref), custom_call_target="tpu_custom_call" | custom-call | flops 4194304 | bytes 524288 | tf_op jit(solution)/shard_map/chip/pallas_call | solution.py:389
  13.4 0.0 copy-start
  13.4 14.0 %all-to-all-start = ((f32[64,1,384]{2,1,0:T(1,128)}), f32[64,1,384]{2,1,0:T(1,128)S(1)}, u32[]{:S(2)}, u32[]{:S(2)}) async-start(f32[64,1,384]{2,1,0:T(1,128)} %get-tuple-element.38), calls=%async_computation | async-start | bytes 196608 | tf_op jit(solution)/shard_map/all_to_all | solution.py:428
  27.4 0.0 copy-done
  27.4 3.2 %inner.1 = (f32[128,1024]{1,0:T(8,128)S(1)}, f32[128,1024]{1,0:T(8,128)S(1)}, f32[16,8,1024]{2,1,0:T(8,128)S(1)}, f32[16,8,1024]{2,1,0:T(8,128)S(1)}, f32[128,128]{1,0:T(8,128)S(1)}, /*index=5*/f32[8,128]{1,0:T(8,128)S(1)}) custom-call(f32[1024,128]{1,0:T(8,128)S(1)} %get-tuple-element.28.u_ref, f32[1024,128]{1,0:T(8,128)S(1)} %get-tuple-element.29.e_ref, ...), custom_call_target="tpu_custom_call" | custom-call | flops 16777216 | bytes 524288 | tf_op jit(solution)/shard_map/inner/pallas_call | solution.py:389
  30.6 4.2 %all-to-all-done.take_ref = f32[64,1,384]{2,1,0:T(1,128)S(1)} async-done(((f32[64,1,384]{2,1,0:T(1,128)}), f32[64,1,384]{2,1,0:T(1,128)S(1)}, u32[]{:S(2)}, u32[]{:S(2)}) %all-to-all-start) | async-done | bytes 98336 | tf_op jit(solution)/shard_map/all_to_all | solution.py:428
  34.8 0.2 chain.1
  35.0 18.5 %all_to_all.10.take_ref = f32[64,1,384]{2,1,0:T(1,128)S(1)} all-to-all(f32[64,1,384]{2,1,0:T(1,128)S(1)} %chain.1), channel_id=1, replica_groups={{320,0,128,256,384,8,136,264,392,16,144,272,400,24,152,280,408,32,160,2..., dimensions={0} | all-to-all | bytes 196608 | tf_op jit(solution)/shard_map/all_to_all | solution.py:440
  53.5 0.1 split.1
  53.6 4.4 %collective-permute-start.1 = (f32[3,64,128]{2,1,0:T(8,128)S(1)}, f32[3,64,128]{2,1,0:T(8,128)S(1)}, u32[]{:S(2)}, u32[]{:S(2)}) collective-permute-start(f32[3,64,128]{2,1,0:T(8,128)S(1)} %get-tuple-element.45), channel_id=1, source_target_pairs={{0,4},{4,0},{8,12},{12,8},{16,20},{20,16},{24,28},{28,24},{32,36},... | collective-permute-start | bytes 294920 | tf_op jit(solution)/shard_map/ppermute | solution.py:446
  58.0 1.4 %own.1 = (f32[128,1024]{1,0:T(8,128)S(1)}, f32[128,1024]{1,0:T(8,128)S(1)}, bf16[4,128,1024]{2,1,0:T(8,128)(2,1)S(1)}) custom-call(s32[1]{0:T(128)} %bitcast.core_ref, bf16[128,1024]{1,0:T(8,128)(2,1)} %q_ref.3, bf16[128,1024]{1,0:T(8,128)(2,1)} %k_ref.3, bf16[128,1024]{1,0:T(8,128)(2,1)} %v_ref.3, bf16[128,1024]{1,0:T(8,128)(2,1)} %dy_ref.3, ...), custom_call_target="tpu_custom_call" | custom-call | flops 4194304 | bytes 524288 | tf_op jit(solution)/shard_map/own/pallas_call | solution.py:389
  59.4 0.0 collective-permute-done.1.got_ref
  59.4 2.4 %mix.1 = (bf16[128,1024]{1,0:T(8,128)(2,1)}, bf16[128,1024]{1,0:T(8,128)(2,1)}, bf16[128,1024]{1,0:T(8,128)(2,1)}, bf16[128,1024]{1,0:T(8,128)(2,1)}, f32[16,1024]{1,0:T(8,128)}) custom-call(s32[1]{0:T(128)} %bitcast.core_ref, bf16[4,128,1024]{2,1,0:T(8,128)(2,1)S(1)} %get-tuple-element.42.inputs_ref, f32[128,1024]{1,0:T(8,128)S(1)} %get-tuple-element.43.conv_ref, ...), custom_call_target="tpu_custom_call" | custom-call | flops 4194304 | bytes 524288 | tf_op jit(solution)/shard_map/mix/pallas_call | solution.py:389
Async XLA Ops:
  3.0 9.7 %collective-permute-start = (f32[3,64,128]{2,1,0:T(8,128)S(1)}, f32[3,64,128]{2,1,0:T(8,128)S(1)}, u32[]{:S(2)}, u32[]{:S(2)}) collective-permute-start(f32[3,64,128]{2,1,0:T(8,128)S(1)} %get-tuple-element.31), channel_id=1, source_target_pairs={{0,4},{4,0},{8,12},{12,8},{16,20},{20,16},{24,28},{28,24},{32,36},... | collective-permute-start | bytes 294920 | tf_op jit(solution)/shard_map/ppermute | solution.py:421
  13.4 14.0 %copy-start = (f32[1024,16]{0,1:T(8,128)S(1)}, f32[1024,16]{0,1:T(8,128)}, u32[]{:S(2)}) copy-start(f32[1024,16]{0,1:T(8,128)} %param.11) | copy-start | bytes 196612
  13.4 21.4 %all-to-all-start = ((f32[64,1,384]{2,1,0:T(1,128)}), f32[64,1,384]{2,1,0:T(1,128)S(1)}, u32[]{:S(2)}, u32[]{:S(2)}) async-start(f32[64,1,384]{2,1,0:T(1,128)} %get-tuple-element.38), calls=%async_computation | async-start | bytes 196608 | tf_op jit(solution)/shard_map/all_to_all | solution.py:428
  53.6 5.8 %collective-permute-start.1 = (f32[3,64,128]{2,1,0:T(8,128)S(1)}, f32[3,64,128]{2,1,0:T(8,128)S(1)}, u32[]{:S(2)}, u32[]{:S(2)}) collective-permute-start(f32[3,64,128]{2,1,0:T(8,128)S(1)} %get-tuple-element.45), channel_id=1, source_target_pairs={{0,4},{4,0},{8,12},{12,8},{16,20},{20,16},{24,28},{28,24},{32,36},... | collective-permute-start | bytes 294920 | tf_op jit(solution)/shard_map/ppermute | solution.py:446

commit v2 on v1

--- a/solution.py
+++ b/solution.py
@@ -9,29 +9,8 @@
 
 LANES = 128
 SUBS = 8
-WIDTH = 4
-DEPTH = 16
-
-
-def listing(first, depths):
-    chips = [x * DEPTH + z for z in depths for x in range(WIDTH)]
-    return [first] + [chip for chip in chips if chip != first]
-
-
-OUT = listing(2 * DEPTH + 11, sorted(range(DEPTH), key=lambda z: min(z, DEPTH - z)))
-BACK = listing(2 * DEPTH + 8, range(DEPTH))
-
-
-def runs(order, start):
-    slots = [order.index(row % WIDTH * DEPTH + row // WIDTH) for row in range(start, start + SUBS)]
-    found = []
-    for place, slot in enumerate(slots):
-        if found and slot == found[-1][1] + found[-1][2]:
-            found[-1][2] += 1
-        else:
-            found.append([place, slot, 1])
-    return found
-CHUNK = 32
+LEAD = 43
+CHUNK = 64
 
 
 def register(ref, index):
@@ -93,8 +72,8 @@
 
 
 def first_kernel(
-    core_ref, q_ref, k_ref, v_ref, dy_ref, dec_ref, theirs_ref, u_ref, e_ref, d_ref,
-    buffers, sems, modes, modes_sem,
+    core_ref, q_ref, k_ref, v_ref, dy_ref, dec_ref, theirs_ref, u_ref, e_ref, d_ref, buffers,
+    sems, modes, modes_sem,
 ):
     rows = q_ref.shape[0]
     modes_copy = pltpu.make_async_copy(dec_ref, modes, modes_sem)
@@ -126,8 +105,9 @@
 def chip_kernel(rows, core_ref, mine_ref, got_ref, d_ref, give_ref, edge_ref, after_ref):
     part = mine_ref.shape[1] // SUBS
     first = core_ref[0] == 0
-    for mode in range(part):
-        place = pl.ds(mode * SUBS, SUBS)
+
+    def body(mode, _):
+        place = pl.ds(pl.multiple_of(mode * SUBS, SUBS), SUBS)
         dec = register(d_ref, core_ref[0] * part + mode)
         span = power(dec, rows)
         here = [mine_ref[which, place, :] for which in range(3)]
@@ -139,18 +119,19 @@
             early[1] + span * late[1],
             early[2] + late[2] + dec * (late[1] * early[0]),
         )
-        for begin, slot, size in runs(OUT, mode * SUBS):
-            for which in range(3):
-                lanes = pl.ds(which * LANES, LANES)
-                give_ref[pl.ds(slot, size), 0, lanes] = joined[which][begin : begin + size]
+        for which in range(3):
+            give_ref[place, 0, pl.ds(which * LANES, LANES)] = joined[which]
         edge_ref[0, place, :] = early[0]
         edge_ref[1, place, :] = late[1]
+        return 0
+
+    lax.fori_loop(0, part, body, 0, unroll=2)
     after_ref[...] = jnp.zeros_like(after_ref)
 
 
 def inner_kernel(
     u_ref, e_ref, d_ref, res_ref, after_ref,
-    conv_ref, rev_ref, lead_ref, trail_ref, leap_ref, ready_ref, r_ref, spun,
+    conv_ref, rev_ref, lead_ref, r_ref, ready_ref, spun,
 ):
     ready_ref[...] = after_ref[...]
     rows = u_ref.shape[0] // SUBS
@@ -189,38 +170,38 @@
 
     sweep(u_ref, conv_ref, 4, 0, 1)
     sweep(e_ref, rev_ref, 4, rows - 1, -1)
-    place = lax.broadcasted_iota(jnp.int32, (SUBS, LANES), 0)
 
     def weights(mode, _):
         for tile in range(SUBS):
-            lanes = pl.ds(tile * LANES, LANES)
-            cell = pl.ds(mode * SUBS + tile, 1)
-            one = jnp.broadcast_to(d_ref[cell, :], place.shape)
-            lead = one * r_ref[cell, :]
-            trail = lead
-            for bit in range(3):
-                lead = jnp.where((place >> bit) & 1 == 1, lead * one, lead)
-                trail = jnp.where((place >> bit) & 1 == 0, trail * one, trail)
-                one = one * one
-            lead_ref[mode, :, lanes] = lead
-            trail_ref[mode, :, lanes] = trail
-            leap_ref[cell, :] = one[:1]
+            lead_ref[mode, :, pl.ds(tile * LANES, LANES)] = eight_rows(mode * SUBS + tile, d_ref, r_ref, 1)[0]
         return 0
 
     lax.fori_loop(0, states, weights, 0)
 
 
-def chain_kernel(rows, core_ref, row_ref, take_ref, d_ref, after_ref, give_ref):
+def eight_rows(cell, d_ref, r_ref, direction):
+    place = lax.broadcasted_iota(jnp.int32, (SUBS, LANES), 0)
+    steps = place if direction == 1 else SUBS - 1 - place
+    base = jnp.broadcast_to(d_ref[pl.ds(cell, 1), :], place.shape)
+    weight = base * r_ref[pl.ds(cell, 1), :]
+    for bit in range(3):
+        weight = jnp.where((steps >> bit) & 1 == 1, weight * base, weight)
+        base = base * base
+    return weight, base
+
+
+def chain_kernel(rows, core_ref, rank_ref, take_ref, d_ref, after_ref, give_ref):
     count = take_ref.shape[0]
-    dec = d_ref[pl.ds(core_ref[0] * count + row_ref[0], 1), :]
+    dec = d_ref[pl.ds(core_ref[0] * count + rank_ref[0], 1), :]
     span = power(dec, 2 * rows)
     zeros = jnp.zeros_like(dec)
     first, second, third = (pl.ds(which * LANES, LANES) for which in range(3))
     before, after, inside, cross = zeros, zeros, zeros, zeros
     for chip in range(count):
-        source, turned = OUT.index(chip), OUT.index(count - 1 - chip)
-        give_ref[BACK.index(chip), :, first] = before
-        give_ref[BACK.index(count - 1 - chip), :, second] = after
+        source = (chip - LEAD) % count
+        turned = (count - 1 - chip - LEAD) % count
+        give_ref[source, :, first] = before
+        give_ref[turned, :, second] = after
         inside = inside + take_ref[source, :, third]
         cross = cross + take_ref[source, :, second] * before
         before = span * before + take_ref[source, :, first]
@@ -230,24 +211,17 @@
         give_ref[block, :, third] = total
 
 
-def split_kernel(rows, core_ref, take_ref, edge_ref, d_ref, keep_ref, pass_ref, sorted_ref):
+def split_kernel(rows, core_ref, take_ref, edge_ref, d_ref, keep_ref, pass_ref):
     part = edge_ref.shape[1] // SUBS
     first = core_ref[0] == 0
-    for mode in range(part):
-        place = pl.ds(mode * SUBS, SUBS)
+
+    def body(mode, _):
+        place = pl.ds(pl.multiple_of(mode * SUBS, SUBS), SUBS)
         dec = register(d_ref, core_ref[0] * part + mode)
         span = power(dec, rows)
-        stretches = runs(BACK, mode * SUBS)
-        found = []
-        for which in range(3):
-            lanes = pl.ds(which * LANES, LANES)
-            if len(stretches) == 1:
-                found.append(take_ref[pl.ds(stretches[0][1], SUBS), 0, lanes])
-                continue
-            for begin, slot, size in stretches:
-                sorted_ref[which, pl.ds(begin, size), :] = take_ref[pl.ds(slot, size), 0, lanes]
-            found.append(sorted_ref[which])
-        start, end, total = found
+        start, end, total = (
+            take_ref[place, 0, pl.ds(which * LANES, LANES)] for which in range(3)
+        )
         middle = span * start + edge_ref[0, place, :]
         turn = span * end + edge_ref[1, place, :]
         keep_ref[0, place, :] = jnp.where(first, start, middle)
@@ -256,15 +230,22 @@
         pass_ref[1, place, :] = jnp.where(first, end, turn)
         keep_ref[2, place, :] = total
         pass_ref[2, place, :] = total
-
-
-def edge_terms(half, table_ref, leap_ref, states_ref, which, tile, lanes):
+        return 0
+
+    lax.fori_loop(0, part, body, 0, unroll=2)
+
+
+def edge_terms(half, lead_ref, d_ref, r_ref, states_ref, which, tile, lanes):
     part = states_ref.shape[1] // SUBS
     terms, leaps = [], []
     for mode in range(part):
         state = states_ref[which, pl.ds(mode * SUBS + tile, 1), :]
-        terms.append(table_ref[half * part + mode, :, lanes] * state)
-        leaps.append(leap_ref[pl.ds((half * part + mode) * SUBS + tile, 1), :])
+        cell = (half * part + mode) * SUBS + tile
+        weight, leap = eight_rows(cell, d_ref, r_ref, 1 if which == 0 else -1)
+        if which == 0:
+            weight = lead_ref[half * part + mode, :, lanes]
+        terms.append(weight * state)
+        leaps.append(leap)
     return terms, leaps
 
 
@@ -275,19 +256,14 @@
 
 
 def own_kernel(
-    core_ref, q_ref, k_ref, v_ref, dy_ref, conv_ref, rev_ref, lead_ref, trail_ref, leap_ref, keep_ref,
-    conv_out, rev_out, inputs_out, sems,
+    core_ref, conv_ref, rev_ref, lead_ref, d_ref, r_ref, keep_ref, conv_out, rev_out
 ):
-    copies = load_copies((q_ref, k_ref, v_ref, dy_ref), inputs_out, sems)
-    for group in copies:
-        for copy in group:
-            copy.start()
     groups = conv_ref.shape[0] // SUBS
 
     def body(tile, _):
         lanes = pl.ds(pl.multiple_of(tile * LANES, LANES), LANES)
-        for which, table, source, out in ((0, lead_ref, conv_ref, conv_out), (1, trail_ref, rev_ref, rev_out)):
-            terms, leaps = edge_terms(core_ref[0], table, leap_ref, keep_ref, which, tile, lanes)
+        for which, source, out in ((0, conv_ref, conv_out), (1, rev_ref, rev_out)):
+            terms, leaps = edge_terms(core_ref[0], lead_ref, d_ref, r_ref, keep_ref, which, tile, lanes)
             for step in range(groups):
                 group = step if which == 0 else groups - 1 - step
                 here = (pl.ds(group * SUBS, SUBS), lanes)
@@ -297,24 +273,18 @@
         return 0
 
     lax.fori_loop(0, SUBS, body, 0)
-    for group in copies:
-        for copy in group:
-            copy.wait()
 
 
 def mix_kernel(
-    core_ref, inputs_ref, conv_ref, rev_ref, lead_ref, trail_ref, leap_ref, keep_ref, got_ref,
+    core_ref, inputs_ref, conv_ref, rev_ref, lead_ref, d_ref, r_ref, keep_ref, got_ref,
     mixed_ref, gq_ref, gk_ref, gv_ref, gr_ref,
-    results, out_sems,
+    results, out_sems, totals, totals_sem,
 ):
     rows = conv_ref.shape[0]
     pairs = rows // (2 * SUBS)
     part = keep_ref.shape[1] // SUBS
     other = 1 - core_ref[0]
-    ways = (
-        (0, lead_ref, conv_ref, (0, 3), (0, 1)),
-        (1, trail_ref, rev_ref, (2, 1), (2, 3)),
-    )
+    ways = ((0, conv_ref, (0, 3), (0, 1)), (1, rev_ref, (2, 1), (2, 3)))
     outs = (mixed_ref, gq_ref, gk_ref, gv_ref)
 
     def leaving(item, tile):
@@ -325,8 +295,8 @@
 
     def body(tile, _):
         lanes = pl.ds(pl.multiple_of(tile * LANES, LANES), LANES)
-        for which, table, source, factors, targets in ways:
-            terms, leaps = edge_terms(other, table, leap_ref, got_ref, which, tile, lanes)
+        for which, source, factors, targets in ways:
+            terms, leaps = edge_terms(other, lead_ref, d_ref, r_ref, got_ref, which, tile, lanes)
             for step in range(pairs):
                 pair = step if which == 0 else pairs - 1 - step
                 halves = []
@@ -345,14 +315,17 @@
                 leaving(target, tile).start()
         return 0
 
-    lax.fori_loop(0, SUBS, body, 0)
     for ref, half in ((keep_ref, core_ref[0]), (got_ref, other)):
         for tile in range(SUBS):
             place = (pl.ds(pl.multiple_of(half * part, SUBS), part), pl.ds(tile * LANES, LANES))
-            gr_ref[place] = ref.at[2][pl.ds(tile, part, stride=SUBS), :]
+            totals[place] = ref.at[2][pl.ds(tile, part, stride=SUBS), :]
+    totals_copy = pltpu.make_async_copy(totals, gr_ref, totals_sem)
+    totals_copy.start()
+    lax.fori_loop(0, SUBS, body, 0)
     for tile in range(SUBS):
         for item in range(len(outs)):
             leaving(item, tile).wait()
+    totals_copy.wait()
 
 
 def local(query, key_gate, value, cotangent, decay, residue):
@@ -364,8 +337,8 @@
     dec = decay.T
     res = residue.T
 
-    def members(order):
-        return [[2 * chip + core for chip in order] for core in range(2)]
+    def members(lead):
+        return [[2 * ((rank + lead) % chips) + core for rank in range(chips)] for core in range(2)]
 
     swap = [(device, device ^ 1) for device in range(count)]
     params = pltpu.CompilerParams(vmem_limit_bytes=24 * 1024 * 1024)
@@ -401,19 +374,17 @@
 
     index = lax.axis_index("ctx").astype(jnp.int32).reshape(1)
     core = index & 1
-    chip = index >> 1
-    row = (chip & (DEPTH - 1)) * WIDTH + chip // DEPTH
+    rank = ((index >> 1) - LEAD) & (chips - 1)
     inputs = [
         pltpu.with_memory_space_constraint(item, pltpu.HBM)
         for item in (query, key_gate, value, cotangent, dec)
     ]
-    loads = pltpu.SemaphoreType.DMA((4, rows // CHUNK))
-    theirs, u, e, modes = run(
+    theirs, u, e, modes, held = run(
         first_kernel, "first",
         [scalar] + [remote] * 5, (core, *inputs),
-        (halved, wide, wide, spread),
+        (halved, wide, wide, spread, four),
         scratch=(
-            pltpu.VMEM(four.shape, four.dtype), loads,
+            pltpu.SemaphoreType.DMA((4, rows // CHUNK)),
             pltpu.VMEM((states, width), jnp.float32), pltpu.SemaphoreType.DMA,
         ),
         work=6,
@@ -425,39 +396,37 @@
         [scalar] + [vector] * 3, (core, mine, got, modes),
         (packed, array(2, cells // 2, LANES), array(SUBS, LANES)),
     )
-    here = lax.all_to_all(send, "ctx", 0, 0, axis_index_groups=members(OUT), tiled=True)
-    conv, rev, lead, trail, leap, ready = run(
+    here = lax.all_to_all(send, "ctx", 0, 0, axis_index_groups=members(LEAD), tiled=True)
+    conv, rev, lead, weights, ready = run(
         inner_kernel, "inner",
         [vector] * 5, (u, e, modes, res, after),
-        (plain, plain, table, table, spread, array(SUBS, LANES)),
-        scratch=(pltpu.VMEM(spread.shape, jnp.float32), pltpu.VMEM(wide.shape, jnp.float32)),
+        (plain, plain, table, spread, array(SUBS, LANES)),
+        scratch=(pltpu.VMEM(wide.shape, jnp.float32),),
         work=8,
     )
     back = run(
         functools.partial(chain_kernel, rows), "chain",
-        [scalar] * 2 + [vector] * 3, (core, row, here, modes, ready), packed,
-    )
-    take = lax.all_to_all(back, "ctx", 0, 0, axis_index_groups=members(BACK), tiled=True)
+        [scalar] * 2 + [vector] * 3, (core, rank, here, modes, ready), packed,
+    )
+    take = lax.all_to_all(back, "ctx", 0, 0, axis_index_groups=members(LEAD), tiled=True)
     keep, away = run(
         functools.partial(split_kernel, rows), "split",
         [scalar] + [vector] * 3, (core, take, edge, modes), (halved, halved),
-        scratch=(pltpu.VMEM((3, SUBS, LANES), jnp.float32),),
     )
     arrived = lax.ppermute(away, "ctx", swap)
-    conv, rev, held = run(
+    conv, rev = run(
         own_kernel, "own",
-        [scalar] + [remote] * 4 + [vector] * 6,
-        (core, *inputs[:4], conv, rev, lead, trail, leap, keep), (plain, plain, four),
-        scratch=(loads,),
+        [scalar] + [vector] * 6, (core, conv, rev, lead, modes, weights, keep), (plain, plain),
     )
     mixed, grad_query, grad_key, grad_value, grad_residue = run(
         mix_kernel, "mix",
         [scalar] + [vector] * 8,
-        (core, held, conv, rev, lead, trail, leap, keep, arrived),
+        (core, held, conv, rev, lead, modes, weights, keep, arrived),
         (block, block, block, block, array(states, width)),
-        out_specs=(remote, remote, remote, remote, vector),
+        out_specs=(remote,) * 5,
         scratch=(
             pltpu.VMEM((4, rows, width), jnp.bfloat16), pltpu.SemaphoreType.DMA((4, SUBS)),
+            pltpu.VMEM((states, width), jnp.float32), pltpu.SemaphoreType.DMA,
         ),
     )
     return (mixed, grad_query, grad_key, grad_value, grad_residue.T)

time: 62.2 us -> 61.1 us (0.982)
  Pallas kernels: 11.1 us -> 9.93 us
  local copies, waits for them, and re-layouts: 0.01 us -> 0.8 us
    pallas_call x8, Pallas kernels: 11.1 us -> 9.93 us  [run(): pl.pallas_call(kernel, out_shape=out_shape, in_specs=specs, out_specs=jax...]
    unnamed x2 -> x6, local copies, waits for them, and re-layouts: 0.01 us -> 0.8 us
  transfers between devices with their start and end apart: 3 -> 3, of which waited for: 1 -> 2; matrix products, arithmetic and copies ran while one was open for 0% -> 0% of each run, Pallas kernels for 9% -> 8%
where the time goes in v2:
time: 61.1 us; the launch traced here: 60.7 us
  starting transfers between devices  27.2 us (45%)
  blocking collectives  17.9 us (29%)
  Pallas kernels  9.93 us (16%)
  waiting for transfers between devices  4.17 us (7%)
  local copies, waits for them, and re-layouts  0.8 us (1%)
  between operations  0.73 us (1%)
    all_to_all x1, blocking collectives, local(): lax.all_to_all(back, 'ctx', 0, 0, axis_index_groups=members(LEAD), tiled=...  17.9 us
    all_to_all x1, starting transfers between devices, local(): lax.all_to_all(send, 'ctx', 0, 0, axis_index_groups=members(LEAD), tiled=...  14 us
    pallas_call x8, Pallas kernels, run(): pl.pallas_call(kernel, out_shape=out_shape, in_specs=specs, out_specs=jax...  9.93 us
    ppermute x1, starting transfers between devices, local(): got = lax.ppermute(theirs, 'ctx', swap)  8.79 us
    ppermute x1, starting transfers between devices, local(): arrived = lax.ppermute(away, 'ctx', swap)  4.4 us
    all_to_all x1, waiting for transfers between devices, local(): lax.all_to_all(send, 'ctx', 0, 0, axis_index_groups=members(LEAD), tiled=...  3.98 us
  transfers between devices with their start and end apart: 3, of which 2 were waited for; matrix products, arithmetic and copies ran while one was open for 0% of the time, Pallas kernels for 8%

profile of v2, /device:TPU:1, one launch (start us, length us, event | category | flops | bytes accessed | tf_op | source)
XLA Modules:
  0.0 60.7 jit_solution(15549989424023573670)
XLA Ops:
  0.6 2.3 %first.1 = (f32[3,64,128]{2,1,0:T(8,128)S(1)}, f32[1024,128]{1,0:T(8,128)S(1)}, f32[1024,128]{1,0:T(8,128)S(1)}, f32[128,128]{1,0:T(8,128)S(1)}, bf16[4,128,1024]{2,1,0:T(8,128)(2,1)S(1)}) custom-call(s32[1]{0:T(128)} %bitcast.core_ref, bf16[128,1024]{1,0:T(8,128)(2,1)} %q_ref.1, bf16[128,1024]{1,0:T(8,128)(2,1)} %k_ref.1, bf16[128,1024]{1,0:T(8,128)(2,1)} %v_ref.1, ...), custom_call_target="tpu_custom_call" | custom-call | flops 12582912 | bytes 524288 | tf_op jit(solution)/shard_map/first/pallas_call | solution.py:362
  3.0 8.8 %collective-permute-start = (f32[3,64,128]{2,1,0:T(8,128)S(1)}, f32[3,64,128]{2,1,0:T(8,128)S(1)}, u32[]{:S(2)}, u32[]{:S(2)}) collective-permute-start(f32[3,64,128]{2,1,0:T(8,128)S(1)} %get-tuple-element.31), channel_id=1, source_target_pairs={{0,4},{4,0},{8,12},{12,8},{16,20},{20,16},{24,28},{28,24},{32,36},... | collective-permute-start | bytes 294920 | tf_op jit(solution)/shard_map/ppermute | solution.py:392
  11.8 0.9 %second.1.mine_ref = f32[3,64,128]{2,1,0:T(8,128)S(1)} custom-call(s32[1]{0:T(128)} %bitcast.core_ref, f32[1024,128]{1,0:T(8,128)S(1)} %get-tuple-element.28.u_ref, f32[1024,128]{1,0:T(8,128)S(1)} %get-tuple-element.29.e_ref, f32[128,128]{1,0:T(8,128)S(1)} %get-tuple-element.30.d_ref), custom_call_target="tpu_custom_call" | custom-call | flops 6291456 | bytes 524288 | tf_op jit(solution)/shard_map/second/pallas_call | solution.py:362
  12.7 0.0 collective-permute-done.got_ref
  12.7 0.7 %chip.1 = (f32[64,1,384]{2,1,0:T(1,128)}, f32[2,64,128]{2,1,0:T(8,128)S(1)}, f32[8,128]{1,0:T(8,128)S(1)}) custom-call(s32[1]{0:T(128)} %bitcast.core_ref, f32[3,64,128]{2,1,0:T(8,128)S(1)} %second.1.mine_ref, f32[3,64,128]{2,1,0:T(8,128)S(1)} %collective-permute-done.got_ref, f32[128,128]{1,0:T(8,128)S(1)} %get-tuple-element.30.d_ref), custom_call_target="tpu_custom_call" | custom-call | flops 4194304 | bytes 524288 | tf_op jit(solution)/shard_map/chip/pallas_call | solution.py:362
  13.5 0.0 copy-start.2
  13.5 14.0 %all-to-all-start = ((f32[64,1,384]{2,1,0:T(1,128)}), f32[64,1,384]{2,1,0:T(1,128)S(1)}, u32[]{:S(2)}, u32[]{:S(2)}) async-start(f32[64,1,384]{2,1,0:T(1,128)} %get-tuple-element.37), calls=%async_computation | async-start | bytes 196608 | tf_op jit(solution)/shard_map/all_to_all | solution.py:399
  27.5 0.0 copy-done.2
  27.5 3.1 %inner.1 = (f32[128,1024]{1,0:T(8,128)S(1)}, f32[128,1024]{1,0:T(8,128)S(1)}, f32[16,8,1024]{2,1,0:T(8,128)S(1)}, f32[128,128]{1,0:T(8,128)S(1)}, f32[8,128]{1,0:T(8,128)S(1)}) custom-call(f32[1024,128]{1,0:T(8,128)S(1)} %get-tuple-element.28.u_ref, f32[1024,128]{1,0:T(8,128)S(1)} %get-tuple-element.29.e_ref, f32[128,128]{1,0:T(8,128)S(1)} %get-tuple-element.30.d_ref, ...), custom_call_target="tpu_custom_call" | custom-call | flops 16777216 | bytes 524288 | tf_op jit(solution)/shard_map/inner/pallas_call | solution.py:362
  30.6 0.0 copy-start
  30.6 0.8 %copy-done = f32[128,1024]{1,0:T(8,128)} copy-done((f32[128,1024]{1,0:T(8,128)}, f32[128,1024]{1,0:T(8,128)S(1)}, u32[]{:S(2)}) %copy-start) | copy-done | bytes 524312
  31.4 4.0 %all-to-all-done.take_ref = f32[64,1,384]{2,1,0:T(1,128)S(1)} async-done(((f32[64,1,384]{2,1,0:T(1,128)}), f32[64,1,384]{2,1,0:T(1,128)S(1)}, u32[]{:S(2)}, u32[]{:S(2)}) %all-to-all-start) | async-done | bytes 98336 | tf_op jit(solution)/shard_map/all_to_all | solution.py:399
  35.4 0.0 copy-start.1
  35.4 0.2 chain.1
  35.5 17.9 %all_to_all.10.take_ref = f32[64,1,384]{2,1,0:T(1,128)S(1)} all-to-all(f32[64,1,384]{2,1,0:T(1,128)S(1)} %chain.1), channel_id=1, replica_groups={{344,352,360,368,376,384,392,400,408,416,424,432,440,448,456,464,472,48..., dimensions={0} | all-to-all | bytes 196608 | tf_op jit(solution)/shard_map/all_to_all | solution.py:411
  53.5 0.1 split.1
  53.5 4.4 %collective-permute-start.1 = (f32[3,64,128]{2,1,0:T(8,128)S(1)}, f32[3,64,128]{2,1,0:T(8,128)S(1)}, u32[]{:S(2)}, u32[]{:S(2)}) collective-permute-start(f32[3,64,128]{2,1,0:T(8,128)S(1)} %get-tuple-element.43), channel_id=1, source_target_pairs={{0,4},{4,0},{8,12},{12,8},{16,20},{20,16},{24,28},{28,24},{32,36},... | collective-permute-start | bytes 294920 | tf_op jit(solution)/shard_map/ppermute | solution.py:416
  58.0 0.0 copy-done.1
  58.0 0.7 %own.1 = (f32[128,1024]{1,0:T(8,128)S(1)}, f32[128,1024]{1,0:T(8,128)S(1)}) custom-call(s32[1]{0:T(128)} %bitcast.core_ref, f32[128,1024]{1,0:T(8,128)S(1)} %get-tuple-element.33.conv_ref, f32[128,1024]{1,0:T(8,128)S(1)} %copy-done.1, f32[16,8,1024]{2,1,0:T(8,128)S(1)} %get-tuple-element.35.lead_ref, f32[128,128]{1,0:T(8,128)S(1)} %get-tuple-element.30.d_ref, ...), custom_call_target="tpu_custom_call" | custom-call | flops 4194304 | bytes 524288 | tf_op jit(solution)/shard_map/own/pallas_call | solution.py:362
  58.7 0.2 collective-permute-done.1.got_ref
  58.9 1.9 %mix.1 = (bf16[128,1024]{1,0:T(8,128)(2,1)}, bf16[128,1024]{1,0:T(8,128)(2,1)}, bf16[128,1024]{1,0:T(8,128)(2,1)}, bf16[128,1024]{1,0:T(8,128)(2,1)}, f32[16,1024]{1,0:T(8,128)}) custom-call(s32[1]{0:T(128)} %bitcast.core_ref, bf16[4,128,1024]{2,1,0:T(8,128)(2,1)S(1)} %get-tuple-element.27.inputs_ref, f32[128,1024]{1,0:T(8,128)S(1)} %get-tuple-element.41.conv_ref, ...), custom_call_target="tpu_custom_call" | custom-call | flops 4194304 | bytes 524288 | tf_op jit(solution)/shard_map/mix/pallas_call | solution.py:362
Async XLA Ops:
  3.0 9.7 %collective-permute-start = (f32[3,64,128]{2,1,0:T(8,128)S(1)}, f32[3,64,128]{2,1,0:T(8,128)S(1)}, u32[]{:S(2)}, u32[]{:S(2)}) collective-permute-start(f32[3,64,128]{2,1,0:T(8,128)S(1)} %get-tuple-element.31), channel_id=1, source_target_pairs={{0,4},{4,0},{8,12},{12,8},{16,20},{20,16},{24,28},{28,24},{32,36},... | collective-permute-start | bytes 294920 | tf_op jit(solution)/shard_map/ppermute | solution.py:392
  13.5 14.0 %copy-start.2 = (f32[1024,16]{0,1:T(8,128)S(1)}, f32[1024,16]{0,1:T(8,128)}, u32[]{:S(2)}) copy-start(f32[1024,16]{0,1:T(8,128)} %param.11) | copy-start | bytes 196612
  13.5 21.9 %all-to-all-start = ((f32[64,1,384]{2,1,0:T(1,128)}), f32[64,1,384]{2,1,0:T(1,128)S(1)}, u32[]{:S(2)}, u32[]{:S(2)}) async-start(f32[64,1,384]{2,1,0:T(1,128)} %get-tuple-element.37), calls=%async_computation | async-start | bytes 196608 | tf_op jit(solution)/shard_map/all_to_all | solution.py:399
  30.6 0.8 %copy-start = (f32[128,1024]{1,0:T(8,128)}, f32[128,1024]{1,0:T(8,128)S(1)}, u32[]{:S(2)}) copy-start(f32[128,1024]{1,0:T(8,128)S(1)} %get-tuple-element.34.rev_ref) | copy-start | bytes 1572868
  35.4 22.6 %copy-start.1 = (f32[128,1024]{1,0:T(8,128)S(1)}, f32[128,1024]{1,0:T(8,128)}, u32[]{:S(2)}) copy-start(f32[128,1024]{1,0:T(8,128)} %copy-done) | copy-start | bytes 1572868
  53.5 5.3 %collective-permute-start.1 = (f32[3,64,128]{2,1,0:T(8,128)S(1)}, f32[3,64,128]{2,1,0:T(8,128)S(1)}, u32[]{:S(2)}, u32[]{:S(2)}) collective-permute-start(f32[3,64,128]{2,1,0:T(8,128)S(1)} %get-tuple-element.43), channel_id=1, source_target_pairs={{0,4},{4,0},{8,12},{12,8},{16,20},{20,16},{24,28},{28,24},{32,36},... | collective-permute-start | bytes 294920 | tf_op jit(solution)/shard_map/ppermute | solution.py:416

commit v3 on v2

--- a/solution.py
+++ b/solution.py
@@ -78,10 +78,12 @@
     rows = q_ref.shape[0]
     modes_copy = pltpu.make_async_copy(dec_ref, modes, modes_sem)
     copies = load_copies((q_ref, k_ref, v_ref, dy_ref), buffers, sems)
+    modes_copy.start()
     for group in copies:
         for copy in group:
             copy.start()
-    modes_copy.start()
+    modes_copy.wait()
+    spread_modes(modes, d_ref)
     for chunk, group in enumerate(copies):
         for copy in group:
             copy.wait()
@@ -93,8 +95,6 @@
                     for half in range(2):
                         start = (row + half * SUBS) * SUBS + tile
                         ref[pl.ds(start, SUBS, stride=SUBS), :] = values[half * SUBS : (half + 1) * SUBS]
-    modes_copy.wait()
-    spread_modes(modes, d_ref)
     end_states(1 - core_ref[0], u_ref, e_ref, d_ref, theirs_ref)
 
 
@@ -102,9 +102,13 @@
     end_states(core_ref[0], u_ref, e_ref, d_ref, mine_ref)
 
 
-def chip_kernel(rows, core_ref, mine_ref, got_ref, d_ref, give_ref, edge_ref, after_ref):
+def chip_kernel(rows, core_ref, mine_ref, got_ref, d_ref, give_ref, edge_ref, after_ref, packed, sems):
     part = mine_ref.shape[1] // SUBS
     first = core_ref[0] == 0
+
+    def leaving(mode):
+        place = pl.ds(mode * SUBS, SUBS)
+        return pltpu.make_async_copy(packed.at[place], give_ref.at[place], sems.at[mode])
 
     def body(mode, _):
         place = pl.ds(pl.multiple_of(mode * SUBS, SUBS), SUBS)
@@ -120,12 +124,15 @@
             early[2] + late[2] + dec * (late[1] * early[0]),
         )
         for which in range(3):
-            give_ref[place, 0, pl.ds(which * LANES, LANES)] = joined[which]
+            packed[place, 0, pl.ds(which * LANES, LANES)] = joined[which]
+        leaving(mode).start()
         edge_ref[0, place, :] = early[0]
         edge_ref[1, place, :] = late[1]
         return 0
 
     lax.fori_loop(0, part, body, 0, unroll=2)
+    for mode in range(part):
+        leaving(mode).wait()
     after_ref[...] = jnp.zeros_like(after_ref)
 
 
@@ -235,7 +242,7 @@
     lax.fori_loop(0, part, body, 0, unroll=2)
 
 
-def edge_terms(half, lead_ref, d_ref, r_ref, states_ref, which, tile, lanes):
+def edge_terms(half, lead_ref, d_ref, r_ref, states_ref, which, tile, lanes, trail_ref=None):
     part = states_ref.shape[1] // SUBS
     terms, leaps = [], []
     for mode in range(part):
@@ -244,6 +251,8 @@
         weight, leap = eight_rows(cell, d_ref, r_ref, 1 if which == 0 else -1)
         if which == 0:
             weight = lead_ref[half * part + mode, :, lanes]
+        elif trail_ref is not None:
+            weight = trail_ref[mode, :, lanes]
         terms.append(weight * state)
         leaps.append(leap)
     return terms, leaps
@@ -256,8 +265,9 @@
 
 
 def own_kernel(
-    core_ref, conv_ref, rev_ref, lead_ref, d_ref, r_ref, keep_ref, conv_out, rev_out
+    core_ref, conv_ref, rev_ref, lead_ref, d_ref, r_ref, keep_ref, conv_out, rev_out, trail_out
 ):
+    part = trail_out.shape[0]
     groups = conv_ref.shape[0] // SUBS
 
     def body(tile, _):
@@ -270,13 +280,16 @@
                 out[here] = source[here] + total_of(terms)
                 if step < groups - 1:
                     terms = [a * b for a, b in zip(terms, leaps)]
+        for mode in range(part):
+            cell = ((1 - core_ref[0]) * part + mode) * SUBS + tile
+            trail_out[mode, :, lanes] = eight_rows(cell, d_ref, r_ref, -1)[0]
         return 0
 
     lax.fori_loop(0, SUBS, body, 0)
 
 
 def mix_kernel(
-    core_ref, inputs_ref, conv_ref, rev_ref, lead_ref, d_ref, r_ref, keep_ref, got_ref,
+    core_ref, inputs_ref, conv_ref, rev_ref, lead_ref, trail_ref, d_ref, r_ref, keep_ref, got_ref,
     mixed_ref, gq_ref, gk_ref, gv_ref, gr_ref,
     results, out_sems, totals, totals_sem,
 ):
@@ -296,7 +309,9 @@
     def body(tile, _):
         lanes = pl.ds(pl.multiple_of(tile * LANES, LANES), LANES)
         for which, source, factors, targets in ways:
-            terms, leaps = edge_terms(other, lead_ref, d_ref, r_ref, got_ref, which, tile, lanes)
+            terms, leaps = edge_terms(
+                other, lead_ref, d_ref, r_ref, got_ref, which, tile, lanes, trail_ref
+            )
             for step in range(pairs):
                 pair = step if which == 0 else pairs - 1 - step
                 halves = []
@@ -394,7 +409,9 @@
     send, edge, after = run(
         functools.partial(chip_kernel, rows), "chip",
         [scalar] + [vector] * 3, (core, mine, got, modes),
-        (packed, array(2, cells // 2, LANES), array(SUBS, LANES)),
+        (pltpu.HBM(packed.shape, packed.dtype), array(2, cells // 2, LANES), array(SUBS, LANES)),
+        out_specs=(remote, vector, vector),
+        scratch=(pltpu.VMEM(packed.shape, jnp.float32), pltpu.SemaphoreType.DMA((states // 2,))),
     )
     here = lax.all_to_all(send, "ctx", 0, 0, axis_index_groups=members(LEAD), tiled=True)
     conv, rev, lead, weights, ready = run(
@@ -414,14 +431,15 @@
         [scalar] + [vector] * 3, (core, take, edge, modes), (halved, halved),
     )
     arrived = lax.ppermute(away, "ctx", swap)
-    conv, rev = run(
+    conv, rev, trail = run(
         own_kernel, "own",
-        [scalar] + [vector] * 6, (core, conv, rev, lead, modes, weights, keep), (plain, plain),
+        [scalar] + [vector] * 6, (core, conv, rev, lead, modes, weights, keep),
+        (plain, plain, array(states // 2, SUBS, width)),
     )
     mixed, grad_query, grad_key, grad_value, grad_residue = run(
         mix_kernel, "mix",
-        [scalar] + [vector] * 8,
-        (core, held, conv, rev, lead, modes, weights, keep, arrived),
+        [scalar] + [vector] * 9,
+        (core, held, conv, rev, lead, trail, modes, weights, keep, arrived),
         (block, block, block, block, array(states, width)),
         out_specs=(remote,) * 5,
         scratch=(

time: 61.1 us -> 61 us (level)
  no operation moved by 1% of the time
where the time goes in v3:
time: 61 us; the launch traced here: 60.7 us
  starting transfers between devices  27.2 us (45%)
  blocking collectives  17.9 us (29%)
  Pallas kernels  9.96 us (16%)
  waiting for transfers between devices  4.11 us (7%)
  local copies, waits for them, and re-layouts  0.81 us (1%)
  between operations  0.75 us (1%)
    all_to_all x1, blocking collectives, local(): lax.all_to_all(back, 'ctx', 0, 0, axis_index_groups=members(LEAD), tiled=...  17.9 us
    all_to_all x1, starting transfers between devices, local(): lax.all_to_all(send, 'ctx', 0, 0, axis_index_groups=members(LEAD), tiled=...  14 us
    pallas_call x8, Pallas kernels, run(): pl.pallas_call(kernel, out_shape=out_shape, in_specs=specs, out_specs=jax...  9.96 us
    ppermute x1, starting transfers between devices, local(): got = lax.ppermute(theirs, 'ctx', swap)  8.79 us
    ppermute x1, starting transfers between devices, local(): arrived = lax.ppermute(away, 'ctx', swap)  4.4 us
    all_to_all x1, waiting for transfers between devices, local(): lax.all_to_all(send, 'ctx', 0, 0, axis_index_groups=members(LEAD), tiled=...  3.98 us
  transfers between devices with their start and end apart: 3, of which 2 were waited for; matrix products, arithmetic and copies ran while one was open for 0% of the time, Pallas kernels for 8%

profile of v3, /device:TPU:1, one launch (start us, length us, event | category | flops | bytes accessed | tf_op | source)
XLA Modules:
  0.0 60.7 jit_solution(6670915917611599006)
XLA Ops:
  0.6 2.4 %first.1 = (f32[3,64,128]{2,1,0:T(8,128)S(1)}, f32[1024,128]{1,0:T(8,128)S(1)}, f32[1024,128]{1,0:T(8,128)S(1)}, f32[128,128]{1,0:T(8,128)S(1)}, bf16[4,128,1024]{2,1,0:T(8,128)(2,1)S(1)}) custom-call(s32[1]{0:T(128)} %bitcast.core_ref, bf16[128,1024]{1,0:T(8,128)(2,1)} %q_ref.1, bf16[128,1024]{1,0:T(8,128)(2,1)} %k_ref.1, bf16[128,1024]{1,0:T(8,128)(2,1)} %v_ref.1, ...), custom_call_target="tpu_custom_call" | custom-call | flops 12582912 | bytes 524288 | tf_op jit(solution)/shard_map/first/pallas_call | solution.py:377
  3.0 8.8 %collective-permute-start = (f32[3,64,128]{2,1,0:T(8,128)S(1)}, f32[3,64,128]{2,1,0:T(8,128)S(1)}, u32[]{:S(2)}, u32[]{:S(2)}) collective-permute-start(f32[3,64,128]{2,1,0:T(8,128)S(1)} %get-tuple-element.32), channel_id=1, source_target_pairs={{0,4},{4,0},{8,12},{12,8},{16,20},{20,16},{24,28},{28,24},{32,36},... | collective-permute-start | bytes 294920 | tf_op jit(solution)/shard_map/ppermute | solution.py:407
  11.8 0.9 %second.1.mine_ref = f32[3,64,128]{2,1,0:T(8,128)S(1)} custom-call(s32[1]{0:T(128)} %bitcast.core_ref, f32[1024,128]{1,0:T(8,128)S(1)} %get-tuple-element.29.u_ref, f32[1024,128]{1,0:T(8,128)S(1)} %get-tuple-element.30.e_ref, f32[128,128]{1,0:T(8,128)S(1)} %get-tuple-element.31.d_ref), custom_call_target="tpu_custom_call" | custom-call | flops 6291456 | bytes 524288 | tf_op jit(solution)/shard_map/second/pallas_call | solution.py:377
  12.7 0.0 collective-permute-done.got_ref
  12.7 0.8 %chip.1 = (f32[64,1,384]{2,1,0:T(1,128)}, f32[2,64,128]{2,1,0:T(8,128)S(1)}, f32[8,128]{1,0:T(8,128)S(1)}) custom-call(s32[1]{0:T(128)} %bitcast.core_ref, f32[3,64,128]{2,1,0:T(8,128)S(1)} %second.1.mine_ref, f32[3,64,128]{2,1,0:T(8,128)S(1)} %collective-permute-done.got_ref, f32[128,128]{1,0:T(8,128)S(1)} %get-tuple-element.31.d_ref), custom_call_target="tpu_custom_call" | custom-call | flops 4194304 | bytes 524288 | tf_op jit(solution)/shard_map/chip/pallas_call | solution.py:377
  13.5 0.0 copy-start.2
  13.5 14.0 %all-to-all-start = ((f32[64,1,384]{2,1,0:T(1,128)}), f32[64,1,384]{2,1,0:T(1,128)S(1)}, u32[]{:S(2)}, u32[]{:S(2)}) async-start(f32[64,1,384]{2,1,0:T(1,128)} %get-tuple-element.38), calls=%async_computation | async-start | bytes 196608 | tf_op jit(solution)/shard_map/all_to_all | solution.py:416
  27.6 0.0 copy-done.2
  27.6 3.1 %inner.1 = (f32[128,1024]{1,0:T(8,128)S(1)}, f32[128,1024]{1,0:T(8,128)S(1)}, f32[16,8,1024]{2,1,0:T(8,128)S(1)}, f32[128,128]{1,0:T(8,128)S(1)}, f32[8,128]{1,0:T(8,128)S(1)}) custom-call(f32[1024,128]{1,0:T(8,128)S(1)} %get-tuple-element.29.u_ref, f32[1024,128]{1,0:T(8,128)S(1)} %get-tuple-element.30.e_ref, f32[128,128]{1,0:T(8,128)S(1)} %get-tuple-element.31.d_ref, ...), custom_call_target="tpu_custom_call" | custom-call | flops 16777216 | bytes 524288 | tf_op jit(solution)/shard_map/inner/pallas_call | solution.py:377
  30.7 0.0 copy-start
  30.7 0.8 %copy-done = f32[128,1024]{1,0:T(8,128)} copy-done((f32[128,1024]{1,0:T(8,128)}, f32[128,1024]{1,0:T(8,128)S(1)}, u32[]{:S(2)}) %copy-start) | copy-done | bytes 524312
  31.5 4.0 %all-to-all-done.take_ref = f32[64,1,384]{2,1,0:T(1,128)S(1)} async-done(((f32[64,1,384]{2,1,0:T(1,128)}), f32[64,1,384]{2,1,0:T(1,128)S(1)}, u32[]{:S(2)}, u32[]{:S(2)}) %all-to-all-start) | async-done | bytes 98336 | tf_op jit(solution)/shard_map/all_to_all | solution.py:416
  35.5 0.0 copy-start.1
  35.5 0.2 chain.1
  35.6 17.9 %all_to_all.10.take_ref = f32[64,1,384]{2,1,0:T(1,128)S(1)} all-to-all(f32[64,1,384]{2,1,0:T(1,128)S(1)} %chain.1), channel_id=1, replica_groups={{344,352,360,368,376,384,392,400,408,416,424,432,440,448,456,464,472,48..., dimensions={0} | all-to-all | bytes 196608 | tf_op jit(solution)/shard_map/all_to_all | solution.py:428
  53.5 0.1 split.1
  53.6 4.4 %collective-permute-start.1 = (f32[3,64,128]{2,1,0:T(8,128)S(1)}, f32[3,64,128]{2,1,0:T(8,128)S(1)}, u32[]{:S(2)}, u32[]{:S(2)}) collective-permute-start(f32[3,64,128]{2,1,0:T(8,128)S(1)} %get-tuple-element.45), channel_id=1, source_target_pairs={{0,4},{4,0},{8,12},{12,8},{16,20},{20,16},{24,28},{28,24},{32,36},... | collective-permute-start | bytes 294920 | tf_op jit(solution)/shard_map/ppermute | solution.py:433
  58.0 0.0 copy-done.1
  58.1 0.8 %own.1 = (f32[128,1024]{1,0:T(8,128)S(1)}, f32[128,1024]{1,0:T(8,128)S(1)}, f32[8,8,1024]{2,1,0:T(8,128)S(1)}) custom-call(s32[1]{0:T(128)} %bitcast.core_ref, f32[128,1024]{1,0:T(8,128)S(1)} %get-tuple-element.34.conv_ref, f32[128,1024]{1,0:T(8,128)S(1)} %copy-done.1, f32[16,8,1024]{2,1,0:T(8,128)S(1)} %get-tuple-element.36.lead_ref, ...), custom_call_target="tpu_custom_call" | custom-call | flops 4194304 | bytes 524288 | tf_op jit(solution)/shard_map/own/pallas_call | solution.py:377
  58.9 0.1 collective-permute-done.1.got_ref
  59.0 1.8 %mix.1 = (bf16[128,1024]{1,0:T(8,128)(2,1)}, bf16[128,1024]{1,0:T(8,128)(2,1)}, bf16[128,1024]{1,0:T(8,128)(2,1)}, bf16[128,1024]{1,0:T(8,128)(2,1)}, f32[16,1024]{1,0:T(8,128)}) custom-call(s32[1]{0:T(128)} %bitcast.core_ref, bf16[4,128,1024]{2,1,0:T(8,128)(2,1)S(1)} %get-tuple-element.28.inputs_ref, f32[128,1024]{1,0:T(8,128)S(1)} %get-tuple-element.42.conv_ref, ...), custom_call_target="tpu_custom_call" | custom-call | flops 4194304 | bytes 524288 | tf_op jit(solution)/shard_map/mix/pallas_call | solution.py:377
Async XLA Ops:
  3.0 9.7 %collective-permute-start = (f32[3,64,128]{2,1,0:T(8,128)S(1)}, f32[3,64,128]{2,1,0:T(8,128)S(1)}, u32[]{:S(2)}, u32[]{:S(2)}) collective-permute-start(f32[3,64,128]{2,1,0:T(8,128)S(1)} %get-tuple-element.32), channel_id=1, source_target_pairs={{0,4},{4,0},{8,12},{12,8},{16,20},{20,16},{24,28},{28,24},{32,36},... | collective-permute-start | bytes 294920 | tf_op jit(solution)/shard_map/ppermute | solution.py:407
  13.5 14.1 %copy-start.2 = (f32[1024,16]{0,1:T(8,128)S(1)}, f32[1024,16]{0,1:T(8,128)}, u32[]{:S(2)}) copy-start(f32[1024,16]{0,1:T(8,128)} %param.11) | copy-start | bytes 196612
  13.5 21.9 %all-to-all-start = ((f32[64,1,384]{2,1,0:T(1,128)}), f32[64,1,384]{2,1,0:T(1,128)S(1)}, u32[]{:S(2)}, u32[]{:S(2)}) async-start(f32[64,1,384]{2,1,0:T(1,128)} %get-tuple-element.38), calls=%async_computation | async-start | bytes 196608 | tf_op jit(solution)/shard_map/all_to_all | solution.py:416
  30.7 0.8 %copy-start = (f32[128,1024]{1,0:T(8,128)}, f32[128,1024]{1,0:T(8,128)S(1)}, u32[]{:S(2)}) copy-start(f32[128,1024]{1,0:T(8,128)S(1)} %get-tuple-element.35.rev_ref) | copy-start | bytes 1572868
  35.5 22.6 %copy-start.1 = (f32[128,1024]{1,0:T(8,128)S(1)}, f32[128,1024]{1,0:T(8,128)}, u32[]{:S(2)}) copy-start(f32[128,1024]{1,0:T(8,128)} %copy-done) | copy-start | bytes 1572868
  53.6 5.3 %collective-permute-start.1 = (f32[3,64,128]{2,1,0:T(8,128)S(1)}, f32[3,64,128]{2,1,0:T(8,128)S(1)}, u32[]{:S(2)}, u32[]{:S(2)}) collective-permute-start(f32[3,64,128]{2,1,0:T(8,128)S(1)} %get-tuple-element.45), channel_id=1, source_target_pairs={{0,4},{4,0},{8,12},{12,8},{16,20},{20,16},{24,28},{28,24},{32,36},... | collective-permute-start | bytes 294920 | tf_op jit(solution)/shard_map/ppermute | solution.py:433

commit v4 on v2

--- a/solution.py
+++ b/solution.py
@@ -9,7 +9,7 @@
 
 LANES = 128
 SUBS = 8
-LEAD = 43
+LEAD = 41
 CHUNK = 64
 
 

time: 61.1 us -> 61.6 us (level)
  waiting for transfers between devices: 4.17 us -> 2.07 us
  blocking collectives: 17.9 us -> 19.4 us
  starting transfers between devices: 27.2 us -> 28.4 us
    all_to_all x1, waiting for transfers between devices: 3.98 us -> 1.88 us  [local(): lax.all_to_all(send, 'ctx', 0, 0, axis_index_groups=members(LEAD), tiled=...]
    all_to_all x1, starting transfers between devices: 14 us -> 15.8 us  [local(): lax.all_to_all(send, 'ctx', 0, 0, axis_index_groups=members(LEAD), tiled=...]
    all_to_all x1, blocking collectives: 17.9 us -> 19.4 us  [local(): lax.all_to_all(back, 'ctx', 0, 0, axis_index_groups=members(LEAD), tiled=...]
where the time goes in v4:
time: 61.6 us; the launch traced here: 61.3 us
  starting transfers between devices  28.4 us (46%)
  blocking collectives  19.4 us (31%)
  Pallas kernels  9.93 us (16%)
  waiting for transfers between devices  2.07 us (3%)
  local copies, waits for them, and re-layouts  0.8 us (1%)
  between operations  0.73 us (1%)
    all_to_all x1, blocking collectives, local(): lax.all_to_all(back, 'ctx', 0, 0, axis_index_groups=members(LEAD), tiled=...  19.4 us
    all_to_all x1, starting transfers between devices, local(): lax.all_to_all(send, 'ctx', 0, 0, axis_index_groups=members(LEAD), tiled=...  15.8 us
    pallas_call x8, Pallas kernels, run(): pl.pallas_call(kernel, out_shape=out_shape, in_specs=specs, out_specs=jax...  9.93 us
    ppermute x1, starting transfers between devices, local(): got = lax.ppermute(theirs, 'ctx', swap)  8.79 us
    ppermute x1, starting transfers between devices, local(): arrived = lax.ppermute(away, 'ctx', swap)  3.8 us
    all_to_all x1, waiting for transfers between devices, local(): lax.all_to_all(send, 'ctx', 0, 0, axis_index_groups=members(LEAD), tiled=...  1.88 us
  transfers between devices with their start and end apart: 3, of which 2 were waited for; matrix products, arithmetic and copies ran while one was open for 0% of the time, Pallas kernels for 8%

profile of v4, /device:TPU:1, one launch (start us, length us, event | category | flops | bytes accessed | tf_op | source)
XLA Modules:
  0.0 61.3 jit_solution(13944288454483109010)
XLA Ops:
  0.6 2.3 %first.1 = (f32[3,64,128]{2,1,0:T(8,128)S(1)}, f32[1024,128]{1,0:T(8,128)S(1)}, f32[1024,128]{1,0:T(8,128)S(1)}, f32[128,128]{1,0:T(8,128)S(1)}, bf16[4,128,1024]{2,1,0:T(8,128)(2,1)S(1)}) custom-call(s32[1]{0:T(128)} %bitcast.core_ref, bf16[128,1024]{1,0:T(8,128)(2,1)} %q_ref.1, bf16[128,1024]{1,0:T(8,128)(2,1)} %k_ref.1, bf16[128,1024]{1,0:T(8,128)(2,1)} %v_ref.1, ...), custom_call_target="tpu_custom_call" | custom-call | flops 12582912 | bytes 524288 | tf_op jit(solution)/shard_map/first/pallas_call | solution.py:362
  3.0 8.8 %collective-permute-start = (f32[3,64,128]{2,1,0:T(8,128)S(1)}, f32[3,64,128]{2,1,0:T(8,128)S(1)}, u32[]{:S(2)}, u32[]{:S(2)}) collective-permute-start(f32[3,64,128]{2,1,0:T(8,128)S(1)} %get-tuple-element.31), channel_id=1, source_target_pairs={{0,4},{4,0},{8,12},{12,8},{16,20},{20,16},{24,28},{28,24},{32,36},... | collective-permute-start | bytes 294920 | tf_op jit(solution)/shard_map/ppermute | solution.py:392
  11.8 0.9 %second.1.mine_ref = f32[3,64,128]{2,1,0:T(8,128)S(1)} custom-call(s32[1]{0:T(128)} %bitcast.core_ref, f32[1024,128]{1,0:T(8,128)S(1)} %get-tuple-element.28.u_ref, f32[1024,128]{1,0:T(8,128)S(1)} %get-tuple-element.29.e_ref, f32[128,128]{1,0:T(8,128)S(1)} %get-tuple-element.30.d_ref), custom_call_target="tpu_custom_call" | custom-call | flops 6291456 | bytes 524288 | tf_op jit(solution)/shard_map/second/pallas_call | solution.py:362
  12.7 0.0 collective-permute-done.got_ref
  12.7 0.7 %chip.1 = (f32[64,1,384]{2,1,0:T(1,128)}, f32[2,64,128]{2,1,0:T(8,128)S(1)}, f32[8,128]{1,0:T(8,128)S(1)}) custom-call(s32[1]{0:T(128)} %bitcast.core_ref, f32[3,64,128]{2,1,0:T(8,128)S(1)} %second.1.mine_ref, f32[3,64,128]{2,1,0:T(8,128)S(1)} %collective-permute-done.got_ref, f32[128,128]{1,0:T(8,128)S(1)} %get-tuple-element.30.d_ref), custom_call_target="tpu_custom_call" | custom-call | flops 4194304 | bytes 524288 | tf_op jit(solution)/shard_map/chip/pallas_call | solution.py:362
  13.5 0.0 copy-start.2
  13.5 15.8 %all-to-all-start = ((f32[64,1,384]{2,1,0:T(1,128)}), f32[64,1,384]{2,1,0:T(1,128)S(1)}, u32[]{:S(2)}, u32[]{:S(2)}) async-start(f32[64,1,384]{2,1,0:T(1,128)} %get-tuple-element.37), calls=%async_computation | async-start | bytes 196608 | tf_op jit(solution)/shard_map/all_to_all | solution.py:399
  29.3 0.0 copy-done.2
  29.3 3.1 %inner.1 = (f32[128,1024]{1,0:T(8,128)S(1)}, f32[128,1024]{1,0:T(8,128)S(1)}, f32[16,8,1024]{2,1,0:T(8,128)S(1)}, f32[128,128]{1,0:T(8,128)S(1)}, f32[8,128]{1,0:T(8,128)S(1)}) custom-call(f32[1024,128]{1,0:T(8,128)S(1)} %get-tuple-element.28.u_ref, f32[1024,128]{1,0:T(8,128)S(1)} %get-tuple-element.29.e_ref, f32[128,128]{1,0:T(8,128)S(1)} %get-tuple-element.30.d_ref, ...), custom_call_target="tpu_custom_call" | custom-call | flops 16777216 | bytes 524288 | tf_op jit(solution)/shard_map/inner/pallas_call | solution.py:362
  32.4 0.0 copy-start
  32.4 0.8 %copy-done = f32[128,1024]{1,0:T(8,128)} copy-done((f32[128,1024]{1,0:T(8,128)}, f32[128,1024]{1,0:T(8,128)S(1)}, u32[]{:S(2)}) %copy-start) | copy-done | bytes 524312
  33.2 1.9 %all-to-all-done.take_ref = f32[64,1,384]{2,1,0:T(1,128)S(1)} async-done(((f32[64,1,384]{2,1,0:T(1,128)}), f32[64,1,384]{2,1,0:T(1,128)S(1)}, u32[]{:S(2)}, u32[]{:S(2)}) %all-to-all-start) | async-done | bytes 98336 | tf_op jit(solution)/shard_map/all_to_all | solution.py:399
  35.1 0.0 copy-start.1
  35.1 0.2 chain.1
  35.3 19.4 %all_to_all.10.take_ref = f32[64,1,384]{2,1,0:T(1,128)S(1)} all-to-all(f32[64,1,384]{2,1,0:T(1,128)S(1)} %chain.1), channel_id=1, replica_groups={{328,336,344,352,360,368,376,384,392,400,408,416,424,432,440,448,456,46..., dimensions={0} | all-to-all | bytes 196608 | tf_op jit(solution)/shard_map/all_to_all | solution.py:411
  54.6 0.1 split.1
  54.7 3.8 %collective-permute-start.1 = (f32[3,64,128]{2,1,0:T(8,128)S(1)}, f32[3,64,128]{2,1,0:T(8,128)S(1)}, u32[]{:S(2)}, u32[]{:S(2)}) collective-permute-start(f32[3,64,128]{2,1,0:T(8,128)S(1)} %get-tuple-element.43), channel_id=1, source_target_pairs={{0,4},{4,0},{8,12},{12,8},{16,20},{20,16},{24,28},{28,24},{32,36},... | collective-permute-start | bytes 294920 | tf_op jit(solution)/shard_map/ppermute | solution.py:416
  58.5 0.0 copy-done.1
  58.5 0.7 %own.1 = (f32[128,1024]{1,0:T(8,128)S(1)}, f32[128,1024]{1,0:T(8,128)S(1)}) custom-call(s32[1]{0:T(128)} %bitcast.core_ref, f32[128,1024]{1,0:T(8,128)S(1)} %get-tuple-element.33.conv_ref, f32[128,1024]{1,0:T(8,128)S(1)} %copy-done.1, f32[16,8,1024]{2,1,0:T(8,128)S(1)} %get-tuple-element.35.lead_ref, f32[128,128]{1,0:T(8,128)S(1)} %get-tuple-element.30.d_ref, ...), custom_call_target="tpu_custom_call" | custom-call | flops 4194304 | bytes 524288 | tf_op jit(solution)/shard_map/own/pallas_call | solution.py:362
  59.3 0.2 collective-permute-done.1.got_ref
  59.4 1.9 %mix.1 = (bf16[128,1024]{1,0:T(8,128)(2,1)}, bf16[128,1024]{1,0:T(8,128)(2,1)}, bf16[128,1024]{1,0:T(8,128)(2,1)}, bf16[128,1024]{1,0:T(8,128)(2,1)}, f32[16,1024]{1,0:T(8,128)}) custom-call(s32[1]{0:T(128)} %bitcast.core_ref, bf16[4,128,1024]{2,1,0:T(8,128)(2,1)S(1)} %get-tuple-element.27.inputs_ref, f32[128,1024]{1,0:T(8,128)S(1)} %get-tuple-element.41.conv_ref, ...), custom_call_target="tpu_custom_call" | custom-call | flops 4194304 | bytes 524288 | tf_op jit(solution)/shard_map/mix/pallas_call | solution.py:362
Async XLA Ops:
  3.0 9.7 %collective-permute-start = (f32[3,64,128]{2,1,0:T(8,128)S(1)}, f32[3,64,128]{2,1,0:T(8,128)S(1)}, u32[]{:S(2)}, u32[]{:S(2)}) collective-permute-start(f32[3,64,128]{2,1,0:T(8,128)S(1)} %get-tuple-element.31), channel_id=1, source_target_pairs={{0,4},{4,0},{8,12},{12,8},{16,20},{20,16},{24,28},{28,24},{32,36},... | collective-permute-start | bytes 294920 | tf_op jit(solution)/shard_map/ppermute | solution.py:392
  13.5 15.8 %copy-start.2 = (f32[1024,16]{0,1:T(8,128)S(1)}, f32[1024,16]{0,1:T(8,128)}, u32[]{:S(2)}) copy-start(f32[1024,16]{0,1:T(8,128)} %param.11) | copy-start | bytes 196612
  13.5 21.6 %all-to-all-start = ((f32[64,1,384]{2,1,0:T(1,128)}), f32[64,1,384]{2,1,0:T(1,128)S(1)}, u32[]{:S(2)}, u32[]{:S(2)}) async-start(f32[64,1,384]{2,1,0:T(1,128)} %get-tuple-element.37), calls=%async_computation | async-start | bytes 196608 | tf_op jit(solution)/shard_map/all_to_all | solution.py:399
  32.4 0.8 %copy-start = (f32[128,1024]{1,0:T(8,128)}, f32[128,1024]{1,0:T(8,128)S(1)}, u32[]{:S(2)}) copy-start(f32[128,1024]{1,0:T(8,128)S(1)} %get-tuple-element.34.rev_ref) | copy-start | bytes 1572868
  35.1 23.4 %copy-start.1 = (f32[128,1024]{1,0:T(8,128)S(1)}, f32[128,1024]{1,0:T(8,128)}, u32[]{:S(2)}) copy-start(f32[128,1024]{1,0:T(8,128)} %copy-done) | copy-start | bytes 1572868
  54.7 4.7 %collective-permute-start.1 = (f32[3,64,128]{2,1,0:T(8,128)S(1)}, f32[3,64,128]{2,1,0:T(8,128)S(1)}, u32[]{:S(2)}, u32[]{:S(2)}) collective-permute-start(f32[3,64,128]{2,1,0:T(8,128)S(1)} %get-tuple-element.43), channel_id=1, source_target_pairs={{0,4},{4,0},{8,12},{12,8},{16,20},{20,16},{24,28},{28,24},{32,36},... | collective-permute-start | bytes 294920 | tf_op jit(solution)/shard_map/ppermute | solution.py:416

commit v5 on v4

--- a/solution.py
+++ b/solution.py
@@ -9,7 +9,7 @@
 
 LANES = 128
 SUBS = 8
-LEAD = 41
+LEAD = 42
 CHUNK = 64
 
 

time: 61.6 us -> 61.3 us (level)
  starting transfers between devices: 28.4 us -> 27 us
  waiting for transfers between devices: 2.07 us -> 3.14 us
    all_to_all x1, waiting for transfers between devices: 1.88 us -> 2.95 us  [local(): lax.all_to_all(send, 'ctx', 0, 0, axis_index_groups=members(LEAD), tiled=...]
    all_to_all x1, starting transfers between devices: 15.8 us -> 14.9 us  [local(): lax.all_to_all(send, 'ctx', 0, 0, axis_index_groups=members(LEAD), tiled=...]
where the time goes in v5:
time: 61.3 us; the launch traced here: 61 us
  starting transfers between devices  27 us (44%)
  blocking collectives  19.4 us (32%)
  Pallas kernels  9.93 us (16%)
  waiting for transfers between devices  3.14 us (5%)
  local copies, waits for them, and re-layouts  0.8 us (1%)
  between operations  0.73 us (1%)
    all_to_all x1, blocking collectives, local(): lax.all_to_all(back, 'ctx', 0, 0, axis_index_groups=members(LEAD), tiled=...  19.4 us
    all_to_all x1, starting transfers between devices, local(): lax.all_to_all(send, 'ctx', 0, 0, axis_index_groups=members(LEAD), tiled=...  14.9 us
    pallas_call x8, Pallas kernels, run(): pl.pallas_call(kernel, out_shape=out_shape, in_specs=specs, out_specs=jax...  9.93 us
    ppermute x1, starting transfers between devices, local(): got = lax.ppermute(theirs, 'ctx', swap)  8.79 us
    ppermute x1, starting transfers between devices, local(): arrived = lax.ppermute(away, 'ctx', swap)  3.32 us
    all_to_all x1, waiting for transfers between devices, local(): lax.all_to_all(send, 'ctx', 0, 0, axis_index_groups=members(LEAD), tiled=...  2.95 us
  transfers between devices with their start and end apart: 3, of which 2 were waited for; matrix products, arithmetic and copies ran while one was open for 0% of the time, Pallas kernels for 8%

profile of v5, /device:TPU:1, one launch (start us, length us, event | category | flops | bytes accessed | tf_op | source)
XLA Modules:
  0.0 61.0 jit_solution(10662610044207752735)
XLA Ops:
  0.6 2.3 %first.1 = (f32[3,64,128]{2,1,0:T(8,128)S(1)}, f32[1024,128]{1,0:T(8,128)S(1)}, f32[1024,128]{1,0:T(8,128)S(1)}, f32[128,128]{1,0:T(8,128)S(1)}, bf16[4,128,1024]{2,1,0:T(8,128)(2,1)S(1)}) custom-call(s32[1]{0:T(128)} %bitcast.core_ref, bf16[128,1024]{1,0:T(8,128)(2,1)} %q_ref.1, bf16[128,1024]{1,0:T(8,128)(2,1)} %k_ref.1, bf16[128,1024]{1,0:T(8,128)(2,1)} %v_ref.1, ...), custom_call_target="tpu_custom_call" | custom-call | flops 12582912 | bytes 524288 | tf_op jit(solution)/shard_map/first/pallas_call | solution.py:362
  3.0 8.8 %collective-permute-start = (f32[3,64,128]{2,1,0:T(8,128)S(1)}, f32[3,64,128]{2,1,0:T(8,128)S(1)}, u32[]{:S(2)}, u32[]{:S(2)}) collective-permute-start(f32[3,64,128]{2,1,0:T(8,128)S(1)} %get-tuple-element.31), channel_id=1, source_target_pairs={{0,4},{4,0},{8,12},{12,8},{16,20},{20,16},{24,28},{28,24},{32,36},... | collective-permute-start | bytes 294920 | tf_op jit(solution)/shard_map/ppermute | solution.py:392
  11.8 0.9 %second.1.mine_ref = f32[3,64,128]{2,1,0:T(8,128)S(1)} custom-call(s32[1]{0:T(128)} %bitcast.core_ref, f32[1024,128]{1,0:T(8,128)S(1)} %get-tuple-element.28.u_ref, f32[1024,128]{1,0:T(8,128)S(1)} %get-tuple-element.29.e_ref, f32[128,128]{1,0:T(8,128)S(1)} %get-tuple-element.30.d_ref), custom_call_target="tpu_custom_call" | custom-call | flops 6291456 | bytes 524288 | tf_op jit(solution)/shard_map/second/pallas_call | solution.py:362
  12.7 0.0 collective-permute-done.got_ref
  12.7 0.7 %chip.1 = (f32[64,1,384]{2,1,0:T(1,128)}, f32[2,64,128]{2,1,0:T(8,128)S(1)}, f32[8,128]{1,0:T(8,128)S(1)}) custom-call(s32[1]{0:T(128)} %bitcast.core_ref, f32[3,64,128]{2,1,0:T(8,128)S(1)} %second.1.mine_ref, f32[3,64,128]{2,1,0:T(8,128)S(1)} %collective-permute-done.got_ref, f32[128,128]{1,0:T(8,128)S(1)} %get-tuple-element.30.d_ref), custom_call_target="tpu_custom_call" | custom-call | flops 4194304 | bytes 524288 | tf_op jit(solution)/shard_map/chip/pallas_call | solution.py:362
  13.5 0.0 copy-start.2
  13.5 14.9 %all-to-all-start = ((f32[64,1,384]{2,1,0:T(1,128)}), f32[64,1,384]{2,1,0:T(1,128)S(1)}, u32[]{:S(2)}, u32[]{:S(2)}) async-start(f32[64,1,384]{2,1,0:T(1,128)} %get-tuple-element.37), calls=%async_computation | async-start | bytes 196608 | tf_op jit(solution)/shard_map/all_to_all | solution.py:399
  28.4 0.0 copy-done.2
  28.4 3.1 %inner.1 = (f32[128,1024]{1,0:T(8,128)S(1)}, f32[128,1024]{1,0:T(8,128)S(1)}, f32[16,8,1024]{2,1,0:T(8,128)S(1)}, f32[128,128]{1,0:T(8,128)S(1)}, f32[8,128]{1,0:T(8,128)S(1)}) custom-call(f32[1024,128]{1,0:T(8,128)S(1)} %get-tuple-element.28.u_ref, f32[1024,128]{1,0:T(8,128)S(1)} %get-tuple-element.29.e_ref, f32[128,128]{1,0:T(8,128)S(1)} %get-tuple-element.30.d_ref, ...), custom_call_target="tpu_custom_call" | custom-call | flops 16777216 | bytes 524288 | tf_op jit(solution)/shard_map/inner/pallas_call | solution.py:362
  31.5 0.0 copy-start
  31.5 0.8 %copy-done = f32[128,1024]{1,0:T(8,128)} copy-done((f32[128,1024]{1,0:T(8,128)}, f32[128,1024]{1,0:T(8,128)S(1)}, u32[]{:S(2)}) %copy-start) | copy-done | bytes 524312
  32.3 3.0 %all-to-all-done.take_ref = f32[64,1,384]{2,1,0:T(1,128)S(1)} async-done(((f32[64,1,384]{2,1,0:T(1,128)}), f32[64,1,384]{2,1,0:T(1,128)S(1)}, u32[]{:S(2)}, u32[]{:S(2)}) %all-to-all-start) | async-done | bytes 98336 | tf_op jit(solution)/shard_map/all_to_all | solution.py:399
  35.2 0.0 copy-start.1
  35.2 0.2 chain.1
  35.4 19.4 %all_to_all.10.take_ref = f32[64,1,384]{2,1,0:T(1,128)S(1)} all-to-all(f32[64,1,384]{2,1,0:T(1,128)S(1)} %chain.1), channel_id=1, replica_groups={{336,344,352,360,368,376,384,392,400,408,416,424,432,440,448,456,464,47..., dimensions={0} | all-to-all | bytes 196608 | tf_op jit(solution)/shard_map/all_to_all | solution.py:411
  54.8 0.1 split.1
  54.9 3.3 %collective-permute-start.1 = (f32[3,64,128]{2,1,0:T(8,128)S(1)}, f32[3,64,128]{2,1,0:T(8,128)S(1)}, u32[]{:S(2)}, u32[]{:S(2)}) collective-permute-start(f32[3,64,128]{2,1,0:T(8,128)S(1)} %get-tuple-element.43), channel_id=1, source_target_pairs={{0,4},{4,0},{8,12},{12,8},{16,20},{20,16},{24,28},{28,24},{32,36},... | collective-permute-start | bytes 294920 | tf_op jit(solution)/shard_map/ppermute | solution.py:416
  58.2 0.0 copy-done.1
  58.3 0.7 %own.1 = (f32[128,1024]{1,0:T(8,128)S(1)}, f32[128,1024]{1,0:T(8,128)S(1)}) custom-call(s32[1]{0:T(128)} %bitcast.core_ref, f32[128,1024]{1,0:T(8,128)S(1)} %get-tuple-element.33.conv_ref, f32[128,1024]{1,0:T(8,128)S(1)} %copy-done.1, f32[16,8,1024]{2,1,0:T(8,128)S(1)} %get-tuple-element.35.lead_ref, f32[128,128]{1,0:T(8,128)S(1)} %get-tuple-element.30.d_ref, ...), custom_call_target="tpu_custom_call" | custom-call | flops 4194304 | bytes 524288 | tf_op jit(solution)/shard_map/own/pallas_call | solution.py:362
  59.0 0.2 collective-permute-done.1.got_ref
  59.2 1.9 %mix.1 = (bf16[128,1024]{1,0:T(8,128)(2,1)}, bf16[128,1024]{1,0:T(8,128)(2,1)}, bf16[128,1024]{1,0:T(8,128)(2,1)}, bf16[128,1024]{1,0:T(8,128)(2,1)}, f32[16,1024]{1,0:T(8,128)}) custom-call(s32[1]{0:T(128)} %bitcast.core_ref, bf16[4,128,1024]{2,1,0:T(8,128)(2,1)S(1)} %get-tuple-element.27.inputs_ref, f32[128,1024]{1,0:T(8,128)S(1)} %get-tuple-element.41.conv_ref, ...), custom_call_target="tpu_custom_call" | custom-call | flops 4194304 | bytes 524288 | tf_op jit(solution)/shard_map/mix/pallas_call | solution.py:362
Async XLA Ops:
  3.0 9.7 %collective-permute-start = (f32[3,64,128]{2,1,0:T(8,128)S(1)}, f32[3,64,128]{2,1,0:T(8,128)S(1)}, u32[]{:S(2)}, u32[]{:S(2)}) collective-permute-start(f32[3,64,128]{2,1,0:T(8,128)S(1)} %get-tuple-element.31), channel_id=1, source_target_pairs={{0,4},{4,0},{8,12},{12,8},{16,20},{20,16},{24,28},{28,24},{32,36},... | collective-permute-start | bytes 294920 | tf_op jit(solution)/shard_map/ppermute | solution.py:392
  13.5 14.9 %copy-start.2 = (f32[1024,16]{0,1:T(8,128)S(1)}, f32[1024,16]{0,1:T(8,128)}, u32[]{:S(2)}) copy-start(f32[1024,16]{0,1:T(8,128)} %param.11) | copy-start | bytes 196612
  13.5 21.8 %all-to-all-start = ((f32[64,1,384]{2,1,0:T(1,128)}), f32[64,1,384]{2,1,0:T(1,128)S(1)}, u32[]{:S(2)}, u32[]{:S(2)}) async-start(f32[64,1,384]{2,1,0:T(1,128)} %get-tuple-element.37), calls=%async_computation | async-start | bytes 196608 | tf_op jit(solution)/shard_map/all_to_all | solution.py:399
  31.5 0.8 %copy-start = (f32[128,1024]{1,0:T(8,128)}, f32[128,1024]{1,0:T(8,128)S(1)}, u32[]{:S(2)}) copy-start(f32[128,1024]{1,0:T(8,128)S(1)} %get-tuple-element.34.rev_ref) | copy-start | bytes 1572868
  35.2 23.0 %copy-start.1 = (f32[128,1024]{1,0:T(8,128)S(1)}, f32[128,1024]{1,0:T(8,128)}, u32[]{:S(2)}) copy-start(f32[128,1024]{1,0:T(8,128)} %copy-done) | copy-start | bytes 1572868
  54.9 4.3 %collective-permute-start.1 = (f32[3,64,128]{2,1,0:T(8,128)S(1)}, f32[3,64,128]{2,1,0:T(8,128)S(1)}, u32[]{:S(2)}, u32[]{:S(2)}) collective-permute-start(f32[3,64,128]{2,1,0:T(8,128)S(1)} %get-tuple-element.43), channel_id=1, source_target_pairs={{0,4},{4,0},{8,12},{12,8},{16,20},{20,16},{24,28},{28,24},{32,36},... | collective-permute-start | bytes 294920 | tf_op jit(solution)/shard_map/ppermute | solution.py:416
